TPU v7x, 512 devices: a whole 4x8x8 slice. The times are simulated.
512 devices in a mesh: pipe: 16 (over z_hi, x, core), expert: 32 (over y, z_lo).
Axes of the slice: x: 4, y: 8, z: 8 (z_hi: 2, z_lo: 4; z = z_hi * 4 + z_lo), core: 2. Of those that a mesh axis runs over, the one named last changes fastest.
Arguments:
- lead_batch: bfloat16 [16, 2048, 3584], P('pipe', 'expert'), may hold values from -6 to 6
- tail_batch: bfloat16 [16, 2048, 3584], P('pipe', 'expert'), may hold values from -6 to 6
- lead_experts: int32 [16, 2048, 1], P('pipe', 'expert'), may hold values from 0 to 3; in each aligned block of 64 rows (0 to 63, 64 to 127, ..., all dimensions but the last counted through in order) at most 17 rows name the same one
- tail_experts: int32 [16, 2048, 1], P('pipe', 'expert'), may hold values from 0 to 3; in each aligned block of 64 rows (0 to 63, 64 to 127, ..., all dimensions but the last counted through in order) at most 17 rows name the same one
- lead_gates: float32 [16, 2048, 1], P('pipe', 'expert'), may hold values from 0.5 to 1.5
- tail_gates: float32 [16, 2048, 1], P('pipe', 'expert'), may hold values from 0.5 to 1.5
- norm_gain: float32 [16, 3584], P('pipe'), may hold values from 0.1 to 1.9
- gate_proj: bfloat16 [16, 3584, 4096], P('pipe', None, 'expert'), may hold values from -0.09375 to 0.09375
- up_proj: bfloat16 [16, 3584, 4096], P('pipe', None, 'expert'), may hold values from -0.09375 to 0.09375
- down_proj: bfloat16 [16, 4096, 3584], P('pipe', 'expert'), may hold values from -0.1875 to 0.1875
Outputs:
- lead_next: bfloat16 [16, 2048, 3584], P('pipe', 'expert')
- tail_next: bfloat16 [16, 2048, 3584], P('pipe', 'expert')
Inputs may be any that keep to these rules, and one draw needn't show every extreme that they name: `lead_experts`: among the 64 tokens of one device in one layer no expert is named more than 17 times, a bound that some block reaches. `tail_experts`: likewise for the tail batch.
All inputs are finite; a program needn't handle non-finite values.
Results may differ from a plain program's by a relative error of at most 0.0095.
Values may be sent and summed in bfloat16 or wider, within the bound.
No kernel may reach another device: no remote copies, remote signals or barrier semaphores. Data moves between devices by JAX's collectives and lax.ppermute only.
A program may use at most 128 MiB of HBM per device.

v0:
```python
import jax
import jax.numpy as jnp
from jax import lax
from jax.sharding import PartitionSpec as P

EXPERTS = 4
CAP = 17


def shifted(shard, axis, by):
    size = lax.axis_size(axis)
    return lax.ppermute(shard, axis, [(i, (i + by) % size) for i in range(size)])


def give_back(partial_value):
    return lax.all_to_all(partial_value, "expert", split_axis=0, concat_axis=0, tiled=True)


def expert_partial(arrived, gate_w, up_w, down_w):
    senders = arrived.shape[0]
    slots = arrived.shape[1]
    flat_rows = arrived.reshape(senders * slots, arrived.shape[2])
    gate_val = jnp.dot(flat_rows, gate_w, preferred_element_type=jnp.float32)
    up_val = jnp.dot(flat_rows, up_w, preferred_element_type=jnp.float32)
    hidden = (jax.nn.silu(gate_val) * up_val).astype(jnp.bfloat16)
    partial_value = jnp.dot(hidden, down_w, preferred_element_type=jnp.float32).astype(jnp.bfloat16)
    return partial_value.reshape(senders, slots, down_w.shape[1])


def layer_step(batch, expert_ids, gates, gain, gate_w, up_w, down_w):
    acts = batch[0]
    width = acts.shape[1]
    shards = lax.axis_size("expert") // EXPERTS
    widened = acts.astype(jnp.float32)
    scale = lax.rsqrt(jnp.mean(widened * widened, axis=-1, keepdims=True) + 1e-06)
    normed = (widened * scale * gain[0][None, :]).astype(jnp.bfloat16)
    experts_of = expert_ids[0, :, 0]
    route_marks = (experts_of[:, None] == jnp.arange(EXPERTS, dtype=jnp.int32)[None, :]).astype(
        jnp.int32
    )
    before_count = jnp.cumsum(route_marks, axis=0) - route_marks
    slot_index = jnp.sum(before_count * route_marks, axis=1)
    dest = experts_of * CAP + slot_index
    placing = (jnp.arange(EXPERTS * CAP, dtype=jnp.int32)[:, None] == dest[None, :]).astype(
        jnp.bfloat16
    )
    buffer = jnp.dot(placing, normed, preferred_element_type=jnp.float32).astype(jnp.bfloat16)
    buffer = buffer.reshape(EXPERTS, CAP, width)
    outgoing = jnp.repeat(buffer, shards, axis=0)
    returned = give_back(
        expert_partial(
            lax.all_to_all(outgoing, "expert", split_axis=0, concat_axis=0, tiled=True),
            gate_w,
            up_w,
            down_w,
        )
    )
    summed = jnp.sum(returned.astype(jnp.float32).reshape(EXPERTS, shards, CAP, width), axis=1)
    branch = jnp.take(summed.reshape(EXPERTS * CAP, width), dest, axis=0)
    result = (widened + gates[0, :, 0:1] * branch).astype(jnp.bfloat16)
    return result[None]


def on_device(
    lead_batch,
    tail_batch,
    lead_experts,
    tail_experts,
    lead_gates,
    tail_gates,
    norm_gain,
    gate_proj,
    up_proj,
    down_proj,
):
    gate_w = gate_proj[0]
    up_w = up_proj[0]
    down_w = down_proj[0]
    lead_out = layer_step(lead_batch, lead_experts, lead_gates, norm_gain, gate_w, up_w, down_w)
    tail_out = layer_step(tail_batch, tail_experts, tail_gates, norm_gain, gate_w, up_w, down_w)
    lead_next = shifted(lead_out, "pipe", 1)
    tail_next = shifted(tail_out, "pipe", -1)
    return (lead_next, tail_next)


def solution(mesh):
    return jax.shard_map(
        on_device,
        mesh=mesh,
        in_specs=(
            P("pipe", "expert", None),
            P("pipe", "expert", None),
            P("pipe", "expert", None),
            P("pipe", "expert", None),
            P("pipe", "expert", None),
            P("pipe", "expert", None),
            P("pipe", None),
            P("pipe", None, "expert"),
            P("pipe", None, "expert"),
            P("pipe", "expert", None),
        ),
        out_specs=(P("pipe", "expert", None), P("pipe", "expert", None)),
        check_vma=False,
    )
```

profile of v0, /device:TPU:7, one launch (start us, length us, event | category | flops | bytes accessed | tf_op | source)
XLA Modules:
  0.0 688.3 jit_solution(17721933909845211488)
XLA Ops:
  0.6 0.0 copy-start
  0.6 0.8 fusion.42
  1.5 0.1 reduce_window_sum.18
  1.5 0.8 select_reduce_fusion
  2.4 0.7 compare_and_fusion
  3.1 1.2 fusion.6
  4.3 0.8 reduce
  5.1 1.4 convolution_convert_fusion.2
  6.4 0.2 reshape.98
  6.6 2.8 broadcast_in_dim.31
  9.4 0.0 copy-start.5
  9.4 0.0 copy-start.2
  9.4 12.9 %all-to-all-start.2 = ((bf16[32,17,3584]{2,1,0:T(8,128)(2,1)}), bf16[32,17,3584]{2,1,0:T(8,128)(2,1)}, u32[]{:S(2)}, u32[]{:S(2)}) async-start(bf16[32,17,3584]{2,1,0:T(8,128)(2,1)} %bitcast.57), calls=%async_computation.2 | async-start | bytes 11010048 | tf_op jit(solution)/shard_map/all_to_all | solution.py:52
  22.3 0.0 copy-done.5
  22.3 0.1 fusion.43
  22.4 0.1 reduce_window_sum.17
  22.5 0.2 select_reduce_fusion.1
  22.6 0.0 copy-done.2
  22.7 0.2 fusion.2
  22.9 0.4 convolution_convert_fusion.3
  23.2 0.2 reshape.91
  23.4 135.7 %all-to-all-done.2 = bf16[32,17,3584]{2,1,0:T(8,128)(2,1)} async-done(((bf16[32,17,3584]{2,1,0:T(8,128)(2,1)}), bf16[32,17,3584]{2,1,0:T(8,128)(2,1)}, u32[]{:S(2)}, u32[]{:S(2)}) %all-to-all-start.2) | async-done | bytes 3899424 | tf_op jit(solution)/shard_map/all_to_all | solution.py:52
  159.1 2.8 broadcast_in_dim.17
  161.8 25.0 %all-to-all-start = ((bf16[32,17,3584]{2,1,0:T(8,128)(2,1)}), bf16[32,17,3584]{2,1,0:T(8,128)(2,1)}, u32[]{:S(2)}, u32[]{:S(2)}) async-start(bf16[32,17,3584]{2,1,0:T(8,128)(2,1)} %bitcast.58), calls=%async_computation | async-start | bytes 11010048 | tf_op jit(solution)/shard_map/all_to_all | solution.py:52
  186.9 0.0 copy-start.8
  186.9 5.6 reshape.100
  192.5 0.0 copy-done.8
  192.5 0.0 copy-start.4
  192.5 3.3 fusion.16
  195.9 0.0 copy-done
  195.9 0.0 copy-done.4
  195.9 8.2 %convolution_convert_fusion = bf16[544,3584]{1,0:T(8,128)(2,1)} fusion(bf16[544,3584]{1,0:T(8,128)(2,1)} %reshape.100, bf16[1,128,3584]{2,1,0:T(8,128)(2,1)S(1)} %copy-done, bf16[1,3584,128]{2,1,0:T(8,128)(2,1)S(1)} %copy-done.4, f32[544,128]{1,0:T(8,128)S(1)} %fusion.16), kind=kOutput, calls=%fused_computation.4 | convolution fusion | flops 1000611840 | bytes 9912320 | tf_op jit(solution)/shard_map/dot_general | solution.py:26
  204.1 5.6 reshape.101
  209.6 123.5 %all-to-all-done = bf16[32,17,3584]{2,1,0:T(8,128)(2,1)} async-done(((bf16[32,17,3584]{2,1,0:T(8,128)(2,1)}), bf16[32,17,3584]{2,1,0:T(8,128)(2,1)}, u32[]{:S(2)}, u32[]{:S(2)}) %all-to-all-start) | async-done | bytes 3899424 | tf_op jit(solution)/shard_map/all_to_all | solution.py:52
  333.1 14.2 %all-to-all-start.3 = ((bf16[32,17,3584]{2,1,0:T(8,128)(2,1)}), bf16[32,17,3584]{2,1,0:T(8,128)(2,1)}, u32[]{:S(2)}, u32[]{:S(2)}) async-start(bf16[32,17,3584]{2,1,0:T(8,128)(2,1)} %reshape.101), calls=%async_computation.3 | async-start | bytes 11010048 | tf_op jit(solution)/shard_map/all_to_all | solution.py:16
  347.3 5.6 reshape.93
  352.9 3.3 fusion.18
  356.1 8.2 %convolution_convert_fusion.1 = bf16[544,3584]{1,0:T(8,128)(2,1)} fusion(bf16[544,3584]{1,0:T(8,128)(2,1)} %reshape.93, bf16[1,128,3584]{2,1,0:T(8,128)(2,1)S(1)} %copy-done, bf16[1,3584,128]{2,1,0:T(8,128)(2,1)S(1)} %copy-done.4, f32[544,128]{1,0:T(8,128)S(1)} %fusion.18), kind=kOutput, calls=%fused_computation.5 | convolution fusion | flops 1000611840 | bytes 9912320 | tf_op jit(solution)/shard_map/dot_general | solution.py:26
  364.3 5.5 reshape.94
  369.8 120.4 %all-to-all-done.3 = bf16[32,17,3584]{2,1,0:T(8,128)(2,1)} async-done(((bf16[32,17,3584]{2,1,0:T(8,128)(2,1)}), bf16[32,17,3584]{2,1,0:T(8,128)(2,1)}, u32[]{:S(2)}, u32[]{:S(2)}) %all-to-all-start.3) | async-done | bytes 3899424 | tf_op jit(solution)/shard_map/all_to_all | solution.py:16
  490.3 19.2 %all-to-all-start.1 = ((bf16[32,17,3584]{2,1,0:T(8,128)(2,1)}), bf16[32,17,3584]{2,1,0:T(8,128)(2,1)}, u32[]{:S(2)}, u32[]{:S(2)}) async-start(bf16[32,17,3584]{2,1,0:T(8,128)(2,1)} %reshape.94), calls=%async_computation.1 | async-start | bytes 11010048 | tf_op jit(solution)/shard_map/all_to_all | solution.py:16
  509.6 3.6 convert_reduce_fusion
  513.1 0.2 reshape.104
  513.3 0.0 copy-start.1
  513.3 0.0 copy-start.6
  513.3 0.9 gather_fusion.1
  514.2 0.1 copy-done.1
  514.3 0.0 copy-done.6
  514.3 1.0 fusion.20
  515.3 2.9 collective-permute-start.1
  518.2 129.6 %all-to-all-done.1 = bf16[32,17,3584]{2,1,0:T(8,128)(2,1)} async-done(((bf16[32,17,3584]{2,1,0:T(8,128)(2,1)}), bf16[32,17,3584]{2,1,0:T(8,128)(2,1)}, u32[]{:S(2)}, u32[]{:S(2)}) %all-to-all-start.1) | async-done | bytes 3899424 | tf_op jit(solution)/shard_map/all_to_all | solution.py:16
  647.7 3.6 convert_reduce_fusion.1
  651.3 0.2 reshape.97
  651.5 0.0 copy-start.3
  651.5 0.0 copy-start.7
  651.5 0.9 gather_fusion
  652.4 0.1 copy-done.3
  652.5 0.0 copy-done.7
  652.5 0.2 fusion.22
  652.7 27.6 %collective-permute-start = (bf16[1,64,3584]{2,1,0:T(8,128)(2,1)S(1)}, bf16[1,64,3584]{2,1,0:T(8,128)(2,1)S(1)}, u32[]{:S(2)}, u32[]{:S(2)}) collective-permute-start(bf16[1,64,3584]{2,1,0:T(8,128)(2,1)S(1)} %fusion.22), channel_id=1, source_target_pairs={{0,32},{32,64},{64,96},{96,128},{128,160},{160,192},{192,224},{224... | collective-permute-start | bytes 1376264 | tf_op jit(solution)/shard_map/ppermute | solution.py:12
  680.3 0.0 collective-permute-done.1
  680.3 5.4 collective-permute-done
  685.7 0.8 copy.14
  686.5 1.8 copy.15
  (7 shorter events, 0.0 us)
Async XLA Ops:
  0.6 195.3 %copy-start = (bf16[1,128,3584]{2,1,0:T(8,128)(2,1)S(1)}, bf16[1,128,3584]{2,1,0:T(8,128)(2,1)}, u32[]{:S(2)}) copy-start(bf16[1,128,3584]{2,1,0:T(8,128)(2,1)} %param.21) | copy-start | bytes 2752516
  9.4 12.9 %copy-start.5 = (s32[1,64,1]{1,2,0:T(1,128)S(1)}, s32[1,64,1]{1,2,0:T(1,128)}, u32[]{:S(2)}) copy-start(s32[1,64,1]{1,2,0:T(1,128)} %param.14) | copy-start | bytes 772
  9.4 13.3 %copy-start.2 = (bf16[1,64,3584]{2,1,0:T(8,128)(2,1)S(1)}, bf16[1,64,3584]{2,1,0:T(8,128)(2,1)}, u32[]{:S(2)}) copy-start(bf16[1,64,3584]{2,1,0:T(8,128)(2,1)} %param.12) | copy-start | bytes 1376260
  9.4 149.7 %all-to-all-start.2 = ((bf16[32,17,3584]{2,1,0:T(8,128)(2,1)}), bf16[32,17,3584]{2,1,0:T(8,128)(2,1)}, u32[]{:S(2)}, u32[]{:S(2)}) async-start(bf16[32,17,3584]{2,1,0:T(8,128)(2,1)} %bitcast.57), calls=%async_computation.2 | async-start | bytes 11010048 | tf_op jit(solution)/shard_map/all_to_all | solution.py:52
  161.8 171.3 %all-to-all-start = ((bf16[32,17,3584]{2,1,0:T(8,128)(2,1)}), bf16[32,17,3584]{2,1,0:T(8,128)(2,1)}, u32[]{:S(2)}, u32[]{:S(2)}) async-start(bf16[32,17,3584]{2,1,0:T(8,128)(2,1)} %bitcast.58), calls=%async_computation | async-start | bytes 11010048 | tf_op jit(solution)/shard_map/all_to_all | solution.py:52
  186.9 5.7 copy-start.8
  192.5 3.4 copy-start.4
  333.1 157.2 %all-to-all-start.3 = ((bf16[32,17,3584]{2,1,0:T(8,128)(2,1)}), bf16[32,17,3584]{2,1,0:T(8,128)(2,1)}, u32[]{:S(2)}, u32[]{:S(2)}) async-start(bf16[32,17,3584]{2,1,0:T(8,128)(2,1)} %reshape.101), calls=%async_computation.3 | async-start | bytes 11010048 | tf_op jit(solution)/shard_map/all_to_all | solution.py:16
  490.3 157.4 %all-to-all-start.1 = ((bf16[32,17,3584]{2,1,0:T(8,128)(2,1)}), bf16[32,17,3584]{2,1,0:T(8,128)(2,1)}, u32[]{:S(2)}, u32[]{:S(2)}) async-start(bf16[32,17,3584]{2,1,0:T(8,128)(2,1)} %reshape.94), calls=%async_computation.1 | async-start | bytes 11010048 | tf_op jit(solution)/shard_map/all_to_all | solution.py:16
  513.3 1.0 copy-start.1
  513.3 1.0 copy-start.6
  515.3 165.0 %collective-permute-start.1 = (bf16[1,64,3584]{2,1,0:T(8,128)(2,1)}, bf16[1,64,3584]{2,1,0:T(8,128)(2,1)}, u32[]{:S(2)}, u32[]{:S(2)}) collective-permute-start(bf16[1,64,3584]{2,1,0:T(8,128)(2,1)} %fusion.20), channel_id=1, source_target_pairs={{0,480},{32,0},{64,32},{96,64},{128,96},{160,128},{192,160},{224,1... | collective-permute-start | bytes 1376264 | tf_op jit(solution)/shard_map/ppermute | solution.py:12
  651.5 1.0 copy-start.3
  651.5 1.0 copy-start.7
  652.7 33.0 %collective-permute-start = (bf16[1,64,3584]{2,1,0:T(8,128)(2,1)S(1)}, bf16[1,64,3584]{2,1,0:T(8,128)(2,1)S(1)}, u32[]{:S(2)}, u32[]{:S(2)}) collective-permute-start(bf16[1,64,3584]{2,1,0:T(8,128)(2,1)S(1)} %fusion.22), channel_id=1, source_target_pairs={{0,32},{32,64},{64,96},{96,128},{128,160},{160,192},{192,224},{224... | collective-permute-start | bytes 1376264 | tf_op jit(solution)/shard_map/ppermute | solution.py:12
where the time goes:
time: 700 us; the launch traced here: 688 us
  waiting for transfers between devices  515 us (74%)
  starting transfers between devices  102 us (15%)
  local copies, waits for them, and re-layouts  33.1 us (5%)
  matrix products  24.7 us (4%)
  other arithmetic  13.3 us (2%)
    all_to_all x2, waiting for transfers between devices, layer_step(): lax.all_to_all(outgoing, 'expert', split_axis=0, concat_axis=0, tiled=True)  259 us
    all_to_all x2, waiting for transfers between devices, give_back(): lax.all_to_all(partial_value, 'expert', split_axis=0, concat_axis=0, tile...  250 us
    all_to_all x2, starting transfers between devices, layer_step(): lax.all_to_all(outgoing, 'expert', split_axis=0, concat_axis=0, tiled=True)  37.9 us
    all_to_all x2, starting transfers between devices, give_back(): lax.all_to_all(partial_value, 'expert', split_axis=0, concat_axis=0, tile...  33.4 us
    ppermute x2, starting transfers between devices, shifted(): lax.ppermute(shard, axis, [(i, (i + by) % size) for i in range(size)])  30.5 us
    dot_general x2, matrix products, expert_partial(): jnp.dot(hidden, down_w, preferred_element_type=jnp.float32)  16.3 us
  transfers between devices with their start and end apart: 6, of which 5 were waited for; matrix products, arithmetic and copies ran while one was open for 8% of the time, Pallas kernels for 0%

commit v1 on v0

v1 whole, which is shorter than its diff:
```python
import functools

import jax
import jax.numpy as jnp
from jax import lax
from jax.experimental import pallas as pl
from jax.experimental.pallas import tpu as pltpu
from jax.sharding import PartitionSpec as P

EXPERTS = 4
CAP = 17
MAIN = 16
RUN = 4
D = 3584
TOK = 64
WIDE = 512
GROUPS = D // WIDE
PART = D // RUN
CUT = 128
CUTS = PART // CUT
SENT = MAIN * GROUPS + 8
BACK = MAIN * CUTS + 8
F32 = jnp.float32
BF16 = jnp.bfloat16
PARAMS = pltpu.CompilerParams(vmem_limit_bytes=40 * 1024 * 1024)


def shifted(shard, axis, by):
    size = lax.axis_size(axis)
    return lax.ppermute(shard, axis, [(i, (i + by) % size) for i in range(size)])


def along_run(shard, by):
    size = lax.axis_size("expert")
    return lax.ppermute(
        shard,
        "expert",
        [(i, i // RUN * RUN + (i + by) % RUN) for i in range(size)],
    )


def with_twin(shard):
    size = lax.axis_size("expert")
    return lax.ppermute(shard, "expert", [(i, i ^ RUN) for i in range(size)])


def placing(expert_row):
    kinds = lax.broadcasted_iota(jnp.int32, (8, TOK), 0)
    marks = kinds == expert_row
    earlier = lax.broadcasted_iota(jnp.int32, (TOK, TOK), 0) < lax.broadcasted_iota(
        jnp.int32, (TOK, TOK), 1
    )
    before = jnp.dot(
        marks.astype(F32).astype(BF16),
        earlier.astype(F32).astype(BF16),
        preferred_element_type=F32,
    )
    slot = jnp.sum(jnp.where(marks, before, 0.0), axis=0, keepdims=True).astype(jnp.int32)
    dest = jnp.where(slot < MAIN, expert_row * MAIN + slot, -1)
    main = lax.broadcasted_iota(jnp.int32, (TOK, TOK), 0) == dest
    last = marks & (slot == MAIN)
    return main.astype(F32).astype(BF16), last.astype(F32).astype(BF16)


def spread_kernel(lead_ref, tail_ref, lead_e_ref, tail_e_ref, gain_ref, out_ref, last_ref):
    for j, (x_ref, e_ref) in enumerate(((lead_ref, lead_e_ref), (tail_ref, tail_e_ref))):
        widened = x_ref[...].astype(F32)
        scale = lax.rsqrt(jnp.mean(widened * widened, axis=-1, keepdims=True) + 1e-06)
        normed = (widened * scale * gain_ref[...]).astype(BF16)
        main, last = placing(e_ref[...])
        rows = jnp.dot(main, normed, preferred_element_type=F32).astype(BF16)
        extra = jnp.dot(last, normed, preferred_element_type=F32)
        last_ref[...] = jnp.zeros_like(last_ref)
        for g in range(GROUPS):
            last_ref[:, g, :] = extra[:, g * WIDE : (g + 1) * WIDE]
            for e in range(EXPERTS):
                out_ref[2 * e + j, g * MAIN : (g + 1) * MAIN, :] = rows[
                    e * MAIN : (e + 1) * MAIN, g * WIDE : (g + 1) * WIDE
                ]
        for e in range(EXPERTS):
            out_ref[2 * e + j, GROUPS * MAIN :, :] = last_ref[e].astype(BF16)


def hidden_kernel(x0, x1, x2, x3, ga, gb, ua, ub, out_ref, acc_ref, last_ref):
    parts = (x0, x1, x2, x3)
    senders = x0.shape[0]
    for k, x in enumerate(parts):
        last_ref[k * senders : (k + 1) * senders] = x[:, GROUPS * MAIN :, :].astype(F32)
    for g in range(GROUPS):
        rows = jnp.concatenate(
            [
                x[:, g * MAIN : (g + 1) * MAIN, :].reshape(senders * MAIN, WIDE)
                for x in parts
            ],
            axis=0,
        )
        rows = jnp.concatenate([rows, last_ref[:, g, :].astype(BF16)], axis=0)
        here = pl.ds(g * WIDE, WIDE)
        for n, (g_w, u_w) in enumerate(((ga, ua), (gb, ub))):
            w = jnp.concatenate([g_w[here, :], u_w[here, :]], axis=1)
            got = jnp.dot(rows, w, preferred_element_type=F32)
            cols = slice(n * 256, (n + 1) * 256)
            if g == 0:
                acc_ref[:, cols] = got
            else:
                acc_ref[:, cols] += got
    for n in range(2):
        gate_val = acc_ref[:, n * 256 : n * 256 + 128]
        up_val = acc_ref[:, n * 256 + 128 : n * 256 + 256]
        out_ref[:, n * 128 : (n + 1) * 128] = (jax.nn.silu(gate_val) * up_val).astype(BF16)


def down_kernel(places, h0, h1, h2, h3, a0, a1, a2, a3, b0, b1, b2, b3, out_ref, last_ref):
    senders = 8
    total = None
    full = RUN * senders * MAIN
    for k, (h, a, b) in enumerate(((h0, a0, b0), (h1, a1, b1), (h2, a2, b2), (h3, a3, b3))):
        w = jnp.concatenate([a[...], b[...]], axis=0)
        got = jnp.dot(h[...], w, preferred_element_type=F32)
        at = full - k * senders * MAIN
        end = full + RUN * senders - k * senders
        if k:
            got = jnp.concatenate([got[at:full], got[:at], got[end:], got[full:end]], axis=0)
        total = got if total is None else total + got
    extra = total[full:]
    rows = total[:full].astype(BF16)
    last_ref[...] = jnp.zeros_like(last_ref)
    for c in range(CUTS):
        last_ref[:, c, :] = extra[:, c * CUT : (c + 1) * CUT]
    for k in range(RUN):
        for y in range(senders):
            place = y * RUN + places[k]
            at = k * senders + y
            for c in range(CUTS):
                out_ref[place, c * MAIN : (c + 1) * MAIN, :] = rows[
                    at * MAIN : (at + 1) * MAIN, c * CUT : (c + 1) * CUT
                ]
            out_ref[place, CUTS * MAIN :, :] = last_ref[at].astype(BF16)


def gather_kernel(j, got_ref, x_ref, e_ref, gate_ref, out_ref, rows_ref, last_ref):
    main, last = placing(e_ref[...])
    last_ref[...] = jnp.zeros_like(last_ref)
    for e in range(EXPERTS):
        for r in range(RUN):
            at = (2 * e + j) * RUN + r
            for c in range(CUTS):
                rows_ref[
                    e * MAIN : (e + 1) * MAIN, r * PART + c * CUT : r * PART + (c + 1) * CUT
                ] = got_ref[at, c * MAIN : (c + 1) * MAIN, :]
            last_ref[e, r * 8 : (r + 1) * 8, :] = got_ref[at, CUTS * MAIN :, :].astype(F32)
    extra = jnp.concatenate(
        [last_ref[:, r * 8 + c, :] for r in range(RUN) for c in range(CUTS)], axis=1
    ).astype(BF16)
    over = (((0,), (0,)), ((), ()))
    branch = lax.dot_general(main, rows_ref[...], over, preferred_element_type=F32)
    branch += lax.dot_general(last, extra, over, preferred_element_type=F32)
    out_ref[...] = (x_ref[...].astype(F32) + gate_ref[...] * branch).astype(BF16)


def call(kernel, shape, dtype, scratch, *args, scalars=0):
    specs = [pl.BlockSpec(memory_space=pltpu.SMEM)] * scalars
    specs += [pl.BlockSpec(memory_space=pltpu.VMEM)] * (len(args) - scalars)
    return pl.pallas_call(
        kernel,
        out_shape=jax.ShapeDtypeStruct(shape, dtype),
        in_specs=specs,
        out_specs=pl.BlockSpec(memory_space=pltpu.VMEM),
        scratch_shapes=[pltpu.VMEM(s, t) for s, t in scratch],
        compiler_params=PARAMS,
    )(*args)


def on_device(
    lead_batch,
    tail_batch,
    lead_experts,
    tail_experts,
    lead_gates,
    tail_gates,
    norm_gain,
    gate_proj,
    up_proj,
    down_proj,
):
    size = lax.axis_size("expert")
    senders = size // RUN
    me = lax.axis_index("expert")
    z = me % RUN
    lead_e = lead_experts[0, :, 0][None, :]
    tail_e = tail_experts[0, :, 0][None, :]
    gate_w, up_w, down_w = gate_proj[0], up_proj[0], down_proj[0]

    cut_w = down_w.reshape(down_w.shape[0], RUN, PART)
    mine = [
        lax.dynamic_index_in_dim(cut_w, (z + k) % RUN, axis=1, keepdims=False)
        for k in range(RUN)
    ]
    down_a = [mine[0]] + [along_run(mine[k], k) for k in range(1, RUN)]

    sent = call(
        spread_kernel,
        (2 * EXPERTS, SENT, WIDE),
        BF16,
        [((8, 8, WIDE), F32)],
        lead_batch[0],
        tail_batch[0],
        lead_e,
        tail_e,
        norm_gain,
    )
    columns = [[y * RUN + r for y in range(senders)] for r in range(RUN)]
    own = lax.all_to_all(sent, "expert", 0, 0, axis_index_groups=columns, tiled=True)
    own, gate_w, up_w, down_a = lax.optimization_barrier((own, gate_w, up_w, down_a))
    xs = [own] + [along_run(own, k) for k in range(1, RUN)]
    gate_b, up_b = with_twin(gate_w), with_twin(up_w)
    down_b = [with_twin(w) for w in down_a]
    rows = RUN * senders * CAP
    hidden = call(
        hidden_kernel,
        (rows, 256),
        BF16,
        [
            ((rows, 512), F32),
            ((RUN * senders, 8, WIDE), F32),
        ],
        *xs,
        gate_w,
        gate_b,
        up_w,
        up_b,
    )
    hs = [hidden] + [along_run(hidden, k) for k in range(1, RUN)]
    places = jnp.stack([(z + RUN - k) % RUN for k in range(RUN)]).astype(jnp.int32)
    back = call(
        down_kernel,
        (size, BACK, CUT),
        BF16,
        [((RUN * senders, 8, CUT), F32)],
        places,
        *hs,
        *down_a,
        *down_b,
        scalars=1,
    )
    got = lax.all_to_all(back, "expert", 0, 0, tiled=True)
    outs = []
    for j, (x, e, gates) in enumerate(
        (
            (lead_batch[0], lead_e, lead_gates[0]),
            (tail_batch[0], tail_e, tail_gates[0]),
        )
    ):
        out = call(
            functools.partial(gather_kernel, j),
            (TOK, D),
            BF16,
            [((TOK, D), BF16), ((8, 8 * RUN, CUT), F32)],
            got,
            x,
            e,
            gates,
        )
        outs.append(shifted(out[None], "pipe", 1 if j == 0 else -1))
    return tuple(outs)


def solution(mesh):
    return jax.shard_map(
        on_device,
        mesh=mesh,
        in_specs=(
            P("pipe", "expert", None),
            P("pipe", "expert", None),
            P("pipe", "expert", None),
            P("pipe", "expert", None),
            P("pipe", "expert", None),
            P("pipe", "expert", None),
            P("pipe", None),
            P("pipe", None, "expert"),
            P("pipe", None, "expert"),
            P("pipe", "expert", None),
        ),
        out_specs=(P("pipe", "expert", None), P("pipe", "expert", None)),
        check_vma=False,
    )
```

time: 700 us -> 240 us (0.34); the launches traced: 688 us -> 239 us
  waiting for transfers between devices: 515 us -> 119 us
  matrix products: 24.7 us -> 0 us
  local copies, waits for them, and re-layouts: 33.1 us -> 11.9 us
  other arithmetic: 13.3 us -> 0.08 us
  Pallas kernels: 0 us -> 8.7 us
    all_to_all x4 -> x2, waiting for transfers between devices: 509 us -> 25.6 us  [the longest x1 23.6 us: on_device(): got = lax.all_to_all(back, 'expert', 0, 0, tiled=True)]
    ppermute x0 -> x15, waiting for transfers between devices: none -> 74.5 us  [the longest x9 43.8 us: along_run(): lax.ppermute(shard, 'expert', [(i, i // RUN * RUN + (i + by) % RUN) for i...]
    ppermute x0 -> x15, starting transfers between devices: none -> 67.6 us  [the longest x9 53.3 us: along_run(): lax.ppermute(shard, 'expert', [(i, i // RUN * RUN + (i + by) % RUN) for i...]
    all_to_all x4 -> x2, starting transfers between devices: 71.3 us -> 17.7 us  [the longest x1 10.7 us: on_device(): got = lax.all_to_all(back, 'expert', 0, 0, tiled=True)]
    dot_general x6 -> x0, matrix products: 24.7 us -> none  [the longest x2 16.3 us: expert_partial(): jnp.dot(hidden, down_w, preferred_element_type=jnp.float32)]
    reshape x8 -> x0, local copies, waits for them, and re-layouts: 22.9 us -> none  [the longest x2 11.2 us: expert_partial(): flat_rows = arrived.reshape(senders * slots, arrived.shape[2])]
    ppermute x2, starting transfers between devices: 30.5 us -> 12.9 us  [shifted(): lax.ppermute(shard, axis, [(i, (i + by) % size) for i in range(size)])]
    ppermute x2, waiting for transfers between devices: 5.39 us -> 18.6 us  [shifted(): lax.ppermute(shard, axis, [(i, (i + by) % size) for i in range(size)])]
  transfers between devices with their start and end apart: 6 -> 19, of which waited for: 5 -> 11; matrix products, arithmetic and copies ran while one was open for 8% -> 1% of each run, Pallas kernels for 0% -> 1%
where the time goes in v1:
time: 240 us; the launch traced here: 239 us
  waiting for transfers between devices  119 us (50%)
  starting transfers between devices  98.2 us (41%)
  local copies, waits for them, and re-layouts  11.9 us (5%)
  Pallas kernels  8.7 us (4%)
    ppermute x9, starting transfers between devices, along_run(): lax.ppermute(shard, 'expert', [(i, i // RUN * RUN + (i + by) % RUN) for i...  53.3 us
    ppermute x9, waiting for transfers between devices, along_run(): lax.ppermute(shard, 'expert', [(i, i // RUN * RUN + (i + by) % RUN) for i...  43.8 us
    ppermute x6, waiting for transfers between devices, with_twin(): return lax.ppermute(shard, 'expert', [(i, i ^ RUN) for i in range(size)])  30.7 us
    all_to_all x1, waiting for transfers between devices, on_device(): got = lax.all_to_all(back, 'expert', 0, 0, tiled=True)  23.6 us
    ppermute x2, waiting for transfers between devices, shifted(): lax.ppermute(shard, axis, [(i, (i + by) % size) for i in range(size)])  18.6 us
    ppermute x6, starting transfers between devices, with_twin(): return lax.ppermute(shard, 'expert', [(i, i ^ RUN) for i in range(size)])  14.3 us
    ppermute x2, starting transfers between devices, shifted(): lax.ppermute(shard, axis, [(i, (i + by) % size) for i in range(size)])  12.9 us
    all_to_all x1, starting transfers between devices, on_device(): got = lax.all_to_all(back, 'expert', 0, 0, tiled=True)  10.7 us
  transfers between devices with their start and end apart: 19, of which 11 were waited for; matrix products, arithmetic and copies ran while one was open for 1% of the time, Pallas kernels for 1%

profile of v1, /device:TPU:7, one launch (start us, length us, event | category | flops | bytes accessed | tf_op | source)
XLA Modules:
  0.0 238.6 jit_solution(117291806191694008)
XLA Ops:
  0.6 0.0 copy-start.11
  0.6 0.0 copy-start.13
  0.7 0.6 copy-done.11
  1.3 0.0 copy-done.13
  1.3 1.0 copy-done
  2.3 1.0 copy-done.2
  3.3 0.7 copy-done.10
  4.1 1.9 shard_map.113
  5.9 6.9 %all-to-all-start = ((bf16[8,120,512]{2,1,0:T(8,128)(2,1)}), bf16[8,120,512]{2,1,0:T(8,128)(2,1)S(1)}, u32[]{:S(2)}, u32[]{:S(2)}) async-start(bf16[8,120,512]{2,1,0:T(8,128)(2,1)} %shard_map.113), calls=%async_computation | async-start | bytes 1966080 | tf_op jit(solution)/shard_map/all_to_all | solution.py:213
  12.9 0.2 reshape_squeeze.3
  13.1 1.9 constant_dynamic-slice_fusion
  15.0 4.0 %collective-permute-start = (bf16[128,896]{1,0:T(8,128)(2,1)S(1)}, bf16[128,896]{1,0:T(8,128)(2,1)S(1)}, u32[]{:S(2)}, u32[]{:S(2)}) collective-permute-start(bf16[128,896]{1,0:T(8,128)(2,1)S(1)} %bitcast.42), channel_id=1, source_target_pairs={{0,1},{1,2},{2,3},{3,0},{4,5},{5,6},{6,7},{7,4},{8,9},{9,10},{10,1... | collective-permute-start | bytes 688136 | tf_op jit(solution)/shard_map/ppermute | solution.py:35
  19.1 0.0 copy-start.4
  19.1 0.0 copy-start.5
  19.1 5.9 %collective-permute-start.1 = (bf16[128,896]{1,0:T(8,128)(2,1)S(1)}, bf16[128,896]{1,0:T(8,128)(2,1)}, u32[]{:S(2)}, u32[]{:S(2)}) collective-permute-start(bf16[128,896]{1,0:T(8,128)(2,1)S(1)} %bitcast.43), channel_id=1, source_target_pairs={{0,2},{1,3},{2,0},{3,1},{4,6},{5,7},{6,4},{7,5},{8,10},{9,11},{10,... | collective-permute-start | bytes 688136 | tf_op jit(solution)/shard_map/ppermute | solution.py:35
  25.1 2.2 collective-permute-start.2
  27.3 0.3 collective-permute-done.a1
  27.7 11.0 %collective-permute-done.1.a2 = bf16[128,896]{1,0:T(8,128)(2,1)} collective-permute-done((bf16[128,896]{1,0:T(8,128)(2,1)S(1)}, bf16[128,896]{1,0:T(8,128)(2,1)}, u32[]{:S(2)}, u32[]{:S(2)}) %collective-permute-start.1) | collective-permute-done | bytes 229408 | tf_op jit(solution)/shard_map/ppermute | solution.py:35
  38.7 0.0 collective-permute-done.2.a3
  38.7 1.9 all-to-all-done.x0
  40.7 1.9 collective-permute-start.6
  42.6 3.4 %collective-permute-start.7 = (bf16[3584,128]{1,0:T(8,128)(2,1)S(1)}, bf16[3584,128]{1,0:T(8,128)(2,1)S(1)}, u32[]{:S(2)}, u32[]{:S(2)}) collective-permute-start(bf16[3584,128]{1,0:T(8,128)(2,1)S(1)} %bitcast.32), channel_id=1, source_target_pairs={{0,4},{1,5},{2,6},{3,7},{4,0},{5,1},{6,2},{7,3},{8,12},{9,13},{10,... | collective-permute-start | bytes 2752520 | tf_op jit(solution)/shard_map/ppermute | solution.py:44
  45.9 5.2 %collective-permute-start.3 = (bf16[8,120,512]{2,1,0:T(8,128)(2,1)S(1)}, bf16[8,120,512]{2,1,0:T(8,128)(2,1)S(1)}, u32[]{:S(2)}, u32[]{:S(2)}) collective-permute-start(bf16[8,120,512]{2,1,0:T(8,128)(2,1)S(1)} %all-to-all-done.x0), channel_id=1, source_target_pairs={{0,1},{1,2},{2,3},{3,0},{4,5},{5,6},{6,7},{7,4},{8,9},{9,10},{10,1... | collective-permute-start | bytes 2949128 | tf_op jit(solution)/shard_map/ppermute | solution.py:35
  51.1 4.6 %collective-permute-start.4 = (bf16[8,120,512]{2,1,0:T(8,128)(2,1)S(1)}, bf16[8,120,512]{2,1,0:T(8,128)(2,1)S(1)}, u32[]{:S(2)}, u32[]{:S(2)}) collective-permute-start(bf16[8,120,512]{2,1,0:T(8,128)(2,1)S(1)} %all-to-all-done.x0), channel_id=1, source_target_pairs={{0,2},{1,3},{2,0},{3,1},{4,6},{5,7},{6,4},{7,5},{8,10},{9,11},{10,... | collective-permute-start | bytes 2949128 | tf_op jit(solution)/shard_map/ppermute | solution.py:35
  55.8 2.2 collective-permute-start.5
  58.0 6.0 %collective-permute-done.6.gb = bf16[3584,128]{1,0:T(8,128)(2,1)S(1)} collective-permute-done((bf16[3584,128]{1,0:T(8,128)(2,1)S(1)}, bf16[3584,128]{1,0:T(8,128)(2,1)S(1)}, u32[]{:S(2)}, u32[]{:S(2)}) %collective-permute-start.6) | collective-permute-done | bytes 917536 | tf_op jit(solution)/shard_map/ppermute | solution.py:44
  64.0 1.9 collective-permute-start.11
  65.9 17.7 %collective-permute-done.7.ub = bf16[3584,128]{1,0:T(8,128)(2,1)S(1)} collective-permute-done((bf16[3584,128]{1,0:T(8,128)(2,1)S(1)}, bf16[3584,128]{1,0:T(8,128)(2,1)S(1)}, u32[]{:S(2)}, u32[]{:S(2)}) %collective-permute-start.7) | collective-permute-done | bytes 917536 | tf_op jit(solution)/shard_map/ppermute | solution.py:44
  83.6 1.9 collective-permute-start.12
  85.5 0.0 collective-permute-done.3.x1
  85.6 32.4 %collective-permute-done.4.x2 = bf16[8,120,512]{2,1,0:T(8,128)(2,1)S(1)} collective-permute-done((bf16[8,120,512]{2,1,0:T(8,128)(2,1)S(1)}, bf16[8,120,512]{2,1,0:T(8,128)(2,1)S(1)}, u32[]{:S(2)}, u32[]{:S(2)}) %collective-permute-start.4) | collective-permute-done | bytes 983072 | tf_op jit(solution)/shard_map/ppermute | solution.py:35
  118.0 2.2 shard_map.114.h0
  120.2 23.3 %collective-permute-start.8 = (bf16[544,256]{1,0:T(8,128)(2,1)S(1)}, bf16[544,256]{1,0:T(8,128)(2,1)S(1)}, u32[]{:S(2)}, u32[]{:S(2)}) collective-permute-start(bf16[544,256]{1,0:T(8,128)(2,1)S(1)} %shard_map.114.h0), channel_id=1, source_target_pairs={{0,1},{1,2},{2,3},{3,0},{4,5},{5,6},{6,7},{7,4},{8,9},{9,10},{10,1... | collective-permute-start | bytes 835592 | tf_op jit(solution)/shard_map/ppermute | solution.py:35
  143.4 1.9 collective-permute-start.9
  145.3 4.0 %collective-permute-start.10 = (bf16[544,256]{1,0:T(8,128)(2,1)S(1)}, bf16[544,256]{1,0:T(8,128)(2,1)S(1)}, u32[]{:S(2)}, u32[]{:S(2)}) collective-permute-start(bf16[544,256]{1,0:T(8,128)(2,1)S(1)} %shard_map.114.h0), channel_id=1, source_target_pairs={{0,3},{1,0},{2,1},{3,2},{4,7},{5,4},{6,5},{7,6},{8,11},{9,8},{10,9... | collective-permute-start | bytes 835592 | tf_op jit(solution)/shard_map/ppermute | solution.py:35
  149.3 0.0 copy-start.6
  149.4 0.7 copy-done.6
  150.0 1.9 collective-permute-start.13
  152.0 0.0 copy-start.8
  152.0 0.7 copy-done.8
  152.7 3.3 %collective-permute-start.14 = (bf16[128,896]{1,0:T(8,128)(2,1)}, bf16[128,896]{1,0:T(8,128)(2,1)S(1)}, u32[]{:S(2)}, u32[]{:S(2)}) collective-permute-start(bf16[128,896]{1,0:T(8,128)(2,1)} %collective-permute-done.2.a3), channel_id=1, source_target_pairs={{0,4},{1,5},{2,6},{3,7},{4,0},{5,1},{6,2},{7,3},{8,12},{9,13},{10,... | collective-permute-start | bytes 688136 | tf_op jit(solution)/shard_map/ppermute | solution.py:44
  156.0 0.1 pad_add_fusion.places
  156.1 2.1 collective-permute-done.13.b2
  158.2 4.9 %collective-permute-done.14.b3 = bf16[128,896]{1,0:T(8,128)(2,1)S(1)} collective-permute-done((bf16[128,896]{1,0:T(8,128)(2,1)}, bf16[128,896]{1,0:T(8,128)(2,1)S(1)}, u32[]{:S(2)}, u32[]{:S(2)}) %collective-permute-start.14) | collective-permute-done | bytes 229408 | tf_op jit(solution)/shard_map/ppermute | solution.py:44
  163.1 0.0 copy-start.7
  163.1 0.9 copy-done.7
  164.0 0.9 copy-done.9
  165.0 3.5 %shard_map.115 = bf16[32,120,128]{2,1,0:T(8,128)(2,1)} custom-call(s32[4]{0:T(128)S(1)} %pad_add_fusion.places, bf16[544,256]{1,0:T(8,128)(2,1)S(1)} %shard_map.114.h0, bf16[544,256]{1,0:T(8,128)(2,1)S(1)} %collective-permute-done.8.h1, bf16[544,256]{1,0:T(8,128)(2,1)S(1)} %collective-permute-done.9.h2, bf16[544,256]{1,0:T(8,128)(2,1)S(1)} %collective-permute-done.10.h3, ...), custom_call_target="tpu_custom_call" | custom-call | tf_op jit(solution)/shard_map/pallas_call | solution.py:164
  168.5 10.7 %all-to-all-start.1 = ((bf16[32,120,128]{2,1,0:T(8,128)(2,1)}), bf16[32,120,128]{2,1,0:T(8,128)(2,1)S(1)}, u32[]{:S(2)}, u32[]{:S(2)}) async-start(bf16[32,120,128]{2,1,0:T(8,128)(2,1)} %shard_map.115), calls=%async_computation.1 | async-start | bytes 1966080 | tf_op jit(solution)/shard_map/all_to_all | solution.py:246
  179.2 0.0 copy-start.16
  179.2 0.6 copy-done.16
  179.8 0.1 copy.16.gate_ref
  179.9 0.7 copy-done.17
  180.6 0.1 copy.17.gate_ref
  180.7 23.6 %all-to-all-done.1.got_ref = bf16[32,120,128]{2,1,0:T(8,128)(2,1)S(1)} async-done(((bf16[32,120,128]{2,1,0:T(8,128)(2,1)}), bf16[32,120,128]{2,1,0:T(8,128)(2,1)S(1)}, u32[]{:S(2)}, u32[]{:S(2)}) %all-to-all-start.1) | async-done | bytes 983072 | tf_op jit(solution)/shard_map/all_to_all | solution.py:246
  204.3 0.6 shard_map.116
  204.9 0.0 copy-start.14
  204.9 11.0 %collective-permute-start.15 = (bf16[1,64,3584]{2,1,0:T(8,128)(2,1)S(1)}, bf16[1,64,3584]{2,1,0:T(8,128)(2,1)S(1)}, u32[]{:S(2)}, u32[]{:S(2)}) collective-permute-start(bf16[1,64,3584]{2,1,0:T(8,128)(2,1)S(1)} %bitcast.36), channel_id=1, source_target_pairs={{0,32},{32,64},{64,96},{96,128},{128,160},{160,192},{192,224},{224... | collective-permute-start | bytes 1376264 | tf_op jit(solution)/shard_map/ppermute | solution.py:30
  215.9 0.6 shard_map.117
  216.5 1.9 collective-permute-start.16
  218.5 7.5 %collective-permute-done.15 = bf16[1,64,3584]{2,1,0:T(8,128)(2,1)S(1)} collective-permute-done((bf16[1,64,3584]{2,1,0:T(8,128)(2,1)S(1)}, bf16[1,64,3584]{2,1,0:T(8,128)(2,1)S(1)}, u32[]{:S(2)}, u32[]{:S(2)}) %collective-permute-start.15) | collective-permute-done | bytes 458784 | tf_op jit(solution)/shard_map/ppermute | solution.py:30
  226.0 11.1 %collective-permute-done.16 = bf16[1,64,3584]{2,1,0:T(8,128)(2,1)S(1)} collective-permute-done((bf16[1,64,3584]{2,1,0:T(8,128)(2,1)S(1)}, bf16[1,64,3584]{2,1,0:T(8,128)(2,1)S(1)}, u32[]{:S(2)}, u32[]{:S(2)}) %collective-permute-start.16) | collective-permute-done | bytes 458784 | tf_op jit(solution)/shard_map/ppermute | solution.py:30
  237.1 0.8 copy.32
  237.8 0.8 copy.33
  (26 shorter events, 0.2 us)
Async XLA Ops:
  0.6 0.7 copy-start.11
  0.6 0.7 copy-start.13
  1.3 1.0 copy-start
  2.3 1.0 copy-start.2
  3.3 0.7 copy-start.10
  5.9 6.9 %copy-start.15 = (bf16[1,128,3584]{2,1,0:T(8,128)(2,1)S(1)}, bf16[1,128,3584]{2,1,0:T(8,128)(2,1)}, u32[]{:S(2)}) copy-start(bf16[1,128,3584]{2,1,0:T(8,128)(2,1)} %param.19) | copy-start | bytes 2752516
  5.9 34.7 %all-to-all-start = ((bf16[8,120,512]{2,1,0:T(8,128)(2,1)}), bf16[8,120,512]{2,1,0:T(8,128)(2,1)S(1)}, u32[]{:S(2)}, u32[]{:S(2)}) async-start(bf16[8,120,512]{2,1,0:T(8,128)(2,1)} %shard_map.113), calls=%async_computation | async-start | bytes 1966080 | tf_op jit(solution)/shard_map/all_to_all | solution.py:213
  15.0 12.6 %collective-permute-start = (bf16[128,896]{1,0:T(8,128)(2,1)S(1)}, bf16[128,896]{1,0:T(8,128)(2,1)S(1)}, u32[]{:S(2)}, u32[]{:S(2)}) collective-permute-start(bf16[128,896]{1,0:T(8,128)(2,1)S(1)} %bitcast.42), channel_id=1, source_target_pairs={{0,1},{1,2},{2,3},{3,0},{4,5},{5,6},{6,7},{7,4},{8,9},{9,10},{10,1... | collective-permute-start | bytes 688136 | tf_op jit(solution)/shard_map/ppermute | solution.py:35
  19.1 21.6 %copy-start.4 = (bf16[1,3584,128]{2,1,0:T(8,128)(2,1)S(1)}, bf16[1,3584,128]{2,1,0:T(8,128)(2,1)}, u32[]{:S(2)}) copy-start(bf16[1,3584,128]{2,1,0:T(8,128)(2,1)} %param.17) | copy-start | bytes 2752516
  19.1 23.5 %copy-start.5 = (bf16[1,3584,128]{2,1,0:T(8,128)(2,1)S(1)}, bf16[1,3584,128]{2,1,0:T(8,128)(2,1)}, u32[]{:S(2)}) copy-start(bf16[1,3584,128]{2,1,0:T(8,128)(2,1)} %param.18) | copy-start | bytes 2752516
  19.1 19.6 %collective-permute-start.1 = (bf16[128,896]{1,0:T(8,128)(2,1)S(1)}, bf16[128,896]{1,0:T(8,128)(2,1)}, u32[]{:S(2)}, u32[]{:S(2)}) collective-permute-start(bf16[128,896]{1,0:T(8,128)(2,1)S(1)} %bitcast.43), channel_id=1, source_target_pairs={{0,2},{1,3},{2,0},{3,1},{4,6},{5,7},{6,4},{7,5},{8,10},{9,11},{10,... | collective-permute-start | bytes 688136 | tf_op jit(solution)/shard_map/ppermute | solution.py:35
  25.1 13.6 %collective-permute-start.2 = (bf16[128,896]{1,0:T(8,128)(2,1)S(1)}, bf16[128,896]{1,0:T(8,128)(2,1)}, u32[]{:S(2)}, u32[]{:S(2)}) collective-permute-start(bf16[128,896]{1,0:T(8,128)(2,1)S(1)} %bitcast.44), channel_id=1, source_target_pairs={{0,3},{1,0},{2,1},{3,2},{4,7},{5,4},{6,5},{7,6},{8,11},{9,8},{10,9... | collective-permute-start | bytes 688136 | tf_op jit(solution)/shard_map/ppermute | solution.py:35
  40.7 23.3 %collective-permute-start.6 = (bf16[3584,128]{1,0:T(8,128)(2,1)S(1)}, bf16[3584,128]{1,0:T(8,128)(2,1)S(1)}, u32[]{:S(2)}, u32[]{:S(2)}) collective-permute-start(bf16[3584,128]{1,0:T(8,128)(2,1)S(1)} %bitcast.30), channel_id=1, source_target_pairs={{0,4},{1,5},{2,6},{3,7},{4,0},{5,1},{6,2},{7,3},{8,12},{9,13},{10,... | collective-permute-start | bytes 2752520 | tf_op jit(solution)/shard_map/ppermute | solution.py:44
  42.6 41.0 %collective-permute-start.7 = (bf16[3584,128]{1,0:T(8,128)(2,1)S(1)}, bf16[3584,128]{1,0:T(8,128)(2,1)S(1)}, u32[]{:S(2)}, u32[]{:S(2)}) collective-permute-start(bf16[3584,128]{1,0:T(8,128)(2,1)S(1)} %bitcast.32), channel_id=1, source_target_pairs={{0,4},{1,5},{2,6},{3,7},{4,0},{5,1},{6,2},{7,3},{8,12},{9,13},{10,... | collective-permute-start | bytes 2752520 | tf_op jit(solution)/shard_map/ppermute | solution.py:44
  45.9 39.6 %collective-permute-start.3 = (bf16[8,120,512]{2,1,0:T(8,128)(2,1)S(1)}, bf16[8,120,512]{2,1,0:T(8,128)(2,1)S(1)}, u32[]{:S(2)}, u32[]{:S(2)}) collective-permute-start(bf16[8,120,512]{2,1,0:T(8,128)(2,1)S(1)} %all-to-all-done.x0), channel_id=1, source_target_pairs={{0,1},{1,2},{2,3},{3,0},{4,5},{5,6},{6,7},{7,4},{8,9},{9,10},{10,1... | collective-permute-start | bytes 2949128 | tf_op jit(solution)/shard_map/ppermute | solution.py:35
  51.1 66.8 %collective-permute-start.4 = (bf16[8,120,512]{2,1,0:T(8,128)(2,1)S(1)}, bf16[8,120,512]{2,1,0:T(8,128)(2,1)S(1)}, u32[]{:S(2)}, u32[]{:S(2)}) collective-permute-start(bf16[8,120,512]{2,1,0:T(8,128)(2,1)S(1)} %all-to-all-done.x0), channel_id=1, source_target_pairs={{0,2},{1,3},{2,0},{3,1},{4,6},{5,7},{6,4},{7,5},{8,10},{9,11},{10,... | collective-permute-start | bytes 2949128 | tf_op jit(solution)/shard_map/ppermute | solution.py:35
  55.8 62.2 %collective-permute-start.5 = (bf16[8,120,512]{2,1,0:T(8,128)(2,1)S(1)}, bf16[8,120,512]{2,1,0:T(8,128)(2,1)S(1)}, u32[]{:S(2)}, u32[]{:S(2)}) collective-permute-start(bf16[8,120,512]{2,1,0:T(8,128)(2,1)S(1)} %all-to-all-done.x0), channel_id=1, source_target_pairs={{0,3},{1,0},{2,1},{3,2},{4,7},{5,4},{6,5},{7,6},{8,11},{9,8},{10,9... | collective-permute-start | bytes 2949128 | tf_op jit(solution)/shard_map/ppermute | solution.py:35
  64.0 85.4 %collective-permute-start.11 = (bf16[128,896]{1,0:T(8,128)(2,1)S(1)}, bf16[128,896]{1,0:T(8,128)(2,1)S(1)}, u32[]{:S(2)}, u32[]{:S(2)}) collective-permute-start(bf16[128,896]{1,0:T(8,128)(2,1)S(1)} %bitcast.34), channel_id=1, source_target_pairs={{0,4},{1,5},{2,6},{3,7},{4,0},{5,1},{6,2},{7,3},{8,12},{9,13},{10,... | collective-permute-start | bytes 688136 | tf_op jit(solution)/shard_map/ppermute | solution.py:44
  83.6 68.3 %collective-permute-start.12 = (bf16[128,896]{1,0:T(8,128)(2,1)S(1)}, bf16[128,896]{1,0:T(8,128)(2,1)S(1)}, u32[]{:S(2)}, u32[]{:S(2)}) collective-permute-start(bf16[128,896]{1,0:T(8,128)(2,1)S(1)} %collective-permute-done.a1), channel_id=1, source_target_pairs={{0,4},{1,5},{2,6},{3,7},{4,0},{5,1},{6,2},{7,3},{8,12},{9,13},{10,... | collective-permute-start | bytes 688136 | tf_op jit(solution)/shard_map/ppermute | solution.py:44
  120.2 42.9 %collective-permute-start.8 = (bf16[544,256]{1,0:T(8,128)(2,1)S(1)}, bf16[544,256]{1,0:T(8,128)(2,1)S(1)}, u32[]{:S(2)}, u32[]{:S(2)}) collective-permute-start(bf16[544,256]{1,0:T(8,128)(2,1)S(1)} %shard_map.114.h0), channel_id=1, source_target_pairs={{0,1},{1,2},{2,3},{3,0},{4,5},{5,6},{6,7},{7,4},{8,9},{9,10},{10,1... | collective-permute-start | bytes 835592 | tf_op jit(solution)/shard_map/ppermute | solution.py:35
  143.4 19.7 %collective-permute-start.9 = (bf16[544,256]{1,0:T(8,128)(2,1)S(1)}, bf16[544,256]{1,0:T(8,128)(2,1)S(1)}, u32[]{:S(2)}, u32[]{:S(2)}) collective-permute-start(bf16[544,256]{1,0:T(8,128)(2,1)S(1)} %shard_map.114.h0), channel_id=1, source_target_pairs={{0,2},{1,3},{2,0},{3,1},{4,6},{5,7},{6,4},{7,5},{8,10},{9,11},{10,... | collective-permute-start | bytes 835592 | tf_op jit(solution)/shard_map/ppermute | solution.py:35
  145.3 17.8 %collective-permute-start.10 = (bf16[544,256]{1,0:T(8,128)(2,1)S(1)}, bf16[544,256]{1,0:T(8,128)(2,1)S(1)}, u32[]{:S(2)}, u32[]{:S(2)}) collective-permute-start(bf16[544,256]{1,0:T(8,128)(2,1)S(1)} %shard_map.114.h0), channel_id=1, source_target_pairs={{0,3},{1,0},{2,1},{3,2},{4,7},{5,4},{6,5},{7,6},{8,11},{9,8},{10,9... | collective-permute-start | bytes 835592 | tf_op jit(solution)/shard_map/ppermute | solution.py:35
  149.3 0.7 copy-start.6
  150.0 8.1 %collective-permute-start.13 = (bf16[128,896]{1,0:T(8,128)(2,1)}, bf16[128,896]{1,0:T(8,128)(2,1)S(1)}, u32[]{:S(2)}, u32[]{:S(2)}) collective-permute-start(bf16[128,896]{1,0:T(8,128)(2,1)} %collective-permute-done.1.a2), channel_id=1, source_target_pairs={{0,4},{1,5},{2,6},{3,7},{4,0},{5,1},{6,2},{7,3},{8,12},{9,13},{10,... | collective-permute-start | bytes 688136 | tf_op jit(solution)/shard_map/ppermute | solution.py:44
  152.0 0.7 copy-start.8
  152.7 10.4 %collective-permute-start.14 = (bf16[128,896]{1,0:T(8,128)(2,1)}, bf16[128,896]{1,0:T(8,128)(2,1)S(1)}, u32[]{:S(2)}, u32[]{:S(2)}) collective-permute-start(bf16[128,896]{1,0:T(8,128)(2,1)} %collective-permute-done.2.a3), channel_id=1, source_target_pairs={{0,4},{1,5},{2,6},{3,7},{4,0},{5,1},{6,2},{7,3},{8,12},{9,13},{10,... | collective-permute-start | bytes 688136 | tf_op jit(solution)/shard_map/ppermute | solution.py:44
  163.1 0.9 copy-start.7
  164.0 0.9 copy-start.9
  168.5 35.9 %copy-start.1 = (bf16[1,64,3584]{2,1,0:T(8,128)(2,1)S(1)}, bf16[1,64,3584]{2,1,0:T(8,128)(2,1)}, u32[]{:S(2)}) copy-start(bf16[1,64,3584]{2,1,0:T(8,128)(2,1)} %param.10) | copy-start | bytes 1376260
  168.5 35.9 %all-to-all-start.1 = ((bf16[32,120,128]{2,1,0:T(8,128)(2,1)}), bf16[32,120,128]{2,1,0:T(8,128)(2,1)S(1)}, u32[]{:S(2)}, u32[]{:S(2)}) async-start(bf16[32,120,128]{2,1,0:T(8,128)(2,1)} %shard_map.115), calls=%async_computation.1 | async-start | bytes 1966080 | tf_op jit(solution)/shard_map/all_to_all | solution.py:246
  179.2 0.7 copy-start.16
  179.9 0.7 copy-start.17
  180.6 23.7 %copy-start.12 = (s32[1,64,1]{1,2,0:T(1,128)S(1)}, s32[1,64,1]{1,2,0:T(1,128)}, u32[]{:S(2)}) copy-start(s32[1,64,1]{1,2,0:T(1,128)} %param.12) | copy-start | bytes 772
  180.7 35.2 %copy-start.3 = (bf16[1,64,3584]{2,1,0:T(8,128)(2,1)S(1)}, bf16[1,64,3584]{2,1,0:T(8,128)(2,1)}, u32[]{:S(2)}) copy-start(bf16[1,64,3584]{2,1,0:T(8,128)(2,1)} %param.11) | copy-start | bytes 1376260
  204.9 11.0 %copy-start.14 = (s32[1,64,1]{1,2,0:T(1,128)S(1)}, s32[1,64,1]{1,2,0:T(1,128)}, u32[]{:S(2)}) copy-start(s32[1,64,1]{1,2,0:T(1,128)} %param.13) | copy-start | bytes 772
  204.9 21.0 %collective-permute-start.15 = (bf16[1,64,3584]{2,1,0:T(8,128)(2,1)S(1)}, bf16[1,64,3584]{2,1,0:T(8,128)(2,1)S(1)}, u32[]{:S(2)}, u32[]{:S(2)}) collective-permute-start(bf16[1,64,3584]{2,1,0:T(8,128)(2,1)S(1)} %bitcast.36), channel_id=1, source_target_pairs={{0,32},{32,64},{64,96},{96,128},{128,160},{160,192},{192,224},{224... | collective-permute-start | bytes 1376264 | tf_op jit(solution)/shard_map/ppermute | solution.py:30
  216.5 20.5 %collective-permute-start.16 = (bf16[1,64,3584]{2,1,0:T(8,128)(2,1)S(1)}, bf16[1,64,3584]{2,1,0:T(8,128)(2,1)S(1)}, u32[]{:S(2)}, u32[]{:S(2)}) collective-permute-start(bf16[1,64,3584]{2,1,0:T(8,128)(2,1)S(1)} %bitcast.37), channel_id=1, source_target_pairs={{0,480},{32,0},{64,32},{96,64},{128,96},{160,128},{192,160},{224,1... | collective-permute-start | bytes 1376264 | tf_op jit(solution)/shard_map/ppermute | solution.py:30

commit v2 on v1

--- a/solution.py
+++ b/solution.py
@@ -11,6 +11,8 @@
 CAP = 17
 MAIN = 16
 RUN = 4
+NEAR = 1
+TEAM = (0, 4, 2, 6)
 D = 3584
 TOK = 64
 WIDE = 512
@@ -30,18 +32,9 @@
     return lax.ppermute(shard, axis, [(i, (i + by) % size) for i in range(size)])
 
 
-def along_run(shard, by):
+def swapped(shard, bits):
     size = lax.axis_size("expert")
-    return lax.ppermute(
-        shard,
-        "expert",
-        [(i, i // RUN * RUN + (i + by) % RUN) for i in range(size)],
-    )
-
-
-def with_twin(shard):
-    size = lax.axis_size("expert")
-    return lax.ppermute(shard, "expert", [(i, i ^ RUN) for i in range(size)])
+    return lax.ppermute(shard, "expert", [(i, i ^ bits) for i in range(size)])
 
 
 def placing(expert_row):
@@ -81,15 +74,16 @@
             out_ref[2 * e + j, GROUPS * MAIN :, :] = last_ref[e].astype(BF16)
 
 
-def hidden_kernel(x0, x1, x2, x3, ga, gb, ua, ub, out_ref, acc_ref, last_ref):
-    parts = (x0, x1, x2, x3)
-    senders = x0.shape[0]
-    for k, x in enumerate(parts):
-        last_ref[k * senders : (k + 1) * senders] = x[:, GROUPS * MAIN :, :].astype(F32)
+def hidden_kernel(*refs):
+    *parts, ga, gb, ua, ub, out_ref, acc_ref, last_ref = refs
+    at = 0
+    for x in parts:
+        last_ref[at : at + x.shape[0]] = x[:, GROUPS * MAIN :, :].astype(F32)
+        at += x.shape[0]
     for g in range(GROUPS):
         rows = jnp.concatenate(
             [
-                x[:, g * MAIN : (g + 1) * MAIN, :].reshape(senders * MAIN, WIDE)
+                x[:, g * MAIN : (g + 1) * MAIN, :].reshape(x.shape[0] * MAIN, WIDE)
                 for x in parts
             ],
             axis=0,
@@ -110,32 +104,38 @@
         out_ref[:, n * 128 : (n + 1) * 128] = (jax.nn.silu(gate_val) * up_val).astype(BF16)
 
 
-def down_kernel(places, h0, h1, h2, h3, a0, a1, a2, a3, b0, b1, b2, b3, out_ref, last_ref):
+def down_kernel(places, *refs):
+    *hs, wa, wb, out_ref, last_ref = refs
     senders = 8
     total = None
     full = RUN * senders * MAIN
-    for k, (h, a, b) in enumerate(((h0, a0, b0), (h1, a1, b1), (h2, a2, b2), (h3, a3, b3))):
-        w = jnp.concatenate([a[...], b[...]], axis=0)
-        got = jnp.dot(h[...], w, preferred_element_type=F32)
-        at = full - k * senders * MAIN
-        end = full + RUN * senders - k * senders
-        if k:
-            got = jnp.concatenate([got[at:full], got[:at], got[end:], got[full:end]], axis=0)
+    block = senders * MAIN
+    for k in range(RUN):
+        w = jnp.concatenate([wa[k], wb[k]], axis=0)
+        got = [jnp.dot(h[...], w, preferred_element_type=F32) for h in hs[2 * k : 2 * k + 2]]
+        main, last = [], []
+        for n in range(RUN):
+            m = n ^ k
+            at = 2 * block + m % 2 * senders
+            main.append(got[m // 2][m % 2 * block : (m % 2 + 1) * block])
+            last.append(got[m // 2][at : at + senders])
+        got = jnp.concatenate(main + last, axis=0)
         total = got if total is None else total + got
     extra = total[full:]
     rows = total[:full].astype(BF16)
     last_ref[...] = jnp.zeros_like(last_ref)
     for c in range(CUTS):
         last_ref[:, c, :] = extra[:, c * CUT : (c + 1) * CUT]
-    for k in range(RUN):
+    for n in range(RUN):
         for y in range(senders):
-            place = y * RUN + places[k]
-            at = k * senders + y
+            place = y * 2 + places[n // 2]
+            batch = places[2 + n % 2]
+            at = n * senders + y
             for c in range(CUTS):
-                out_ref[place, c * MAIN : (c + 1) * MAIN, :] = rows[
+                out_ref[place, batch, c * MAIN : (c + 1) * MAIN, :] = rows[
                     at * MAIN : (at + 1) * MAIN, c * CUT : (c + 1) * CUT
                 ]
-            out_ref[place, CUTS * MAIN :, :] = last_ref[at].astype(BF16)
+            out_ref[place, batch, CUTS * MAIN :, :] = last_ref[at].astype(BF16)
 
 
 def gather_kernel(j, got_ref, x_ref, e_ref, gate_ref, out_ref, rows_ref, last_ref):
@@ -143,12 +143,12 @@
     last_ref[...] = jnp.zeros_like(last_ref)
     for e in range(EXPERTS):
         for r in range(RUN):
-            at = (2 * e + j) * RUN + r
+            at = e * RUN + r
             for c in range(CUTS):
                 rows_ref[
                     e * MAIN : (e + 1) * MAIN, r * PART + c * CUT : r * PART + (c + 1) * CUT
-                ] = got_ref[at, c * MAIN : (c + 1) * MAIN, :]
-            last_ref[e, r * 8 : (r + 1) * 8, :] = got_ref[at, CUTS * MAIN :, :].astype(F32)
+                ] = got_ref[at, j, c * MAIN : (c + 1) * MAIN, :]
+            last_ref[e, r * 8 : (r + 1) * 8, :] = got_ref[at, j, CUTS * MAIN :, :].astype(F32)
     extra = jnp.concatenate(
         [last_ref[:, r * 8 + c, :] for r in range(RUN) for c in range(CUTS)], axis=1
     ).astype(BF16)
@@ -169,6 +169,18 @@
         scratch_shapes=[pltpu.VMEM(s, t) for s, t in scratch],
         compiler_params=PARAMS,
     )(*args)
+
+
+def hidden_of(parts, weights):
+    rows = sum(part.shape[0] for part in parts)
+    return call(
+        hidden_kernel,
+        (rows * CAP, 256),
+        BF16,
+        [((rows * CAP, 512), F32), ((rows, 8, WIDE), F32)],
+        *parts,
+        *weights,
+    )
 
 
 def on_device(
@@ -186,17 +198,25 @@
     size = lax.axis_size("expert")
     senders = size // RUN
     me = lax.axis_index("expert")
-    z = me % RUN
+    twin, far = me // RUN % 2, me % RUN // 2
     lead_e = lead_experts[0, :, 0][None, :]
     tail_e = tail_experts[0, :, 0][None, :]
     gate_w, up_w, down_w = gate_proj[0], up_proj[0], down_proj[0]
-
-    cut_w = down_w.reshape(down_w.shape[0], RUN, PART)
-    mine = [
-        lax.dynamic_index_in_dim(cut_w, (z + k) % RUN, axis=1, keepdims=False)
-        for k in range(RUN)
-    ]
-    down_a = [mine[0]] + [along_run(mine[k], k) for k in range(1, RUN)]
+    gate_b, up_b = swapped(gate_w, NEAR), swapped(up_w, NEAR)
+
+    cuts = [down_w[:, n * PART : (n + 1) * PART] for n in range(RUN)]
+    mine = 2 * twin + far
+    parts = []
+    for k in range(RUN):
+        flip = k % 2 * 2 + k // 2
+        parts.append(
+            jnp.where(
+                mine < 2,
+                jnp.where(mine == 0, cuts[flip], cuts[1 ^ flip]),
+                jnp.where(mine == 2, cuts[2 ^ flip], cuts[3 ^ flip]),
+            )
+        )
+    from_far = swapped(jnp.stack(parts[2:]), TEAM[2])
 
     sent = call(
         spread_kernel,
@@ -211,39 +231,41 @@
     )
     columns = [[y * RUN + r for y in range(senders)] for r in range(RUN)]
     own = lax.all_to_all(sent, "expert", 0, 0, axis_index_groups=columns, tiled=True)
-    own, gate_w, up_w, down_a = lax.optimization_barrier((own, gate_w, up_w, down_a))
-    xs = [own] + [along_run(own, k) for k in range(1, RUN)]
-    gate_b, up_b = with_twin(gate_w), with_twin(up_w)
-    down_b = [with_twin(w) for w in down_a]
-    rows = RUN * senders * CAP
-    hidden = call(
-        hidden_kernel,
-        (rows, 256),
-        BF16,
-        [
-            ((rows, 512), F32),
-            ((RUN * senders, 8, WIDE), F32),
-        ],
-        *xs,
-        gate_w,
-        gate_b,
-        up_w,
-        up_b,
-    )
-    hs = [hidden] + [along_run(hidden, k) for k in range(1, RUN)]
-    places = jnp.stack([(z + RUN - k) % RUN for k in range(RUN)]).astype(jnp.int32)
+    step = lax.optimization_barrier
+    own, gate_b, from_far = step((own, gate_b, from_far))
+    half = senders // 2
+    near_rows, far_rows = swapped(own[:half], TEAM[2]), swapped(own[half:], TEAM[2])
+    beside = swapped(own, TEAM[1])
+    from_twin = swapped(jnp.stack([parts[1], from_far[1]]), TEAM[1])
+    beside, from_twin = step((beside, from_twin))
+    weights = (gate_w, gate_b, up_w, up_b)
+    early = hidden_of((own, beside), weights)
+    down_a = jnp.stack([parts[0], from_twin[0], from_far[0], from_twin[1]])
+    early, down_a = step((early, down_a))
+    down_b = swapped(down_a, NEAR)
+    early_sent = [swapped(early, TEAM[k]) for k in range(1, RUN)]
+    near_last, far_last = swapped(near_rows, TEAM[1]), swapped(far_rows, TEAM[1])
+    far_last, early_sent = step((far_last, early_sent))
+    late = hidden_of((near_rows, far_rows, near_last, far_last), weights)
+    hs = [early, late]
+    for k in range(1, RUN):
+        hs += [early_sent[k - 1], swapped(late, TEAM[k])]
+    places = jnp.stack([far, far ^ 1, twin, twin ^ 1]).astype(jnp.int32)
     back = call(
         down_kernel,
-        (size, BACK, CUT),
+        (size // 2, 2, BACK, CUT),
         BF16,
         [((RUN * senders, 8, CUT), F32)],
         places,
         *hs,
-        *down_a,
-        *down_b,
+        down_a,
+        down_b,
         scalars=1,
     )
-    got = lax.all_to_all(back, "expert", 0, 0, tiled=True)
+    halves = [
+        [y * RUN + n + 2 * f for y in range(senders) for f in range(2)] for n in range(2)
+    ]
+    got = lax.all_to_all(back, "expert", 0, 0, axis_index_groups=halves, tiled=True)
     outs = []
     for j, (x, e, gates) in enumerate(
         (

time: 240 us -> 218 us (0.908)
  starting transfers between devices: 98.2 us -> 84.2 us
  waiting for transfers between devices: 119 us -> 112 us
  local copies, waits for them, and re-layouts: 11.9 us -> 6.62 us
  Pallas kernels: 8.7 us -> 11.4 us
    ppermute x15 -> x16, starting transfers between devices: 67.6 us -> 52.7 us  [swapped(): return lax.ppermute(shard, 'expert', [(i, i ^ bits) for i in range(size)])]
    ppermute x2, starting transfers between devices: 12.9 us -> 17.8 us  [shifted(): lax.ppermute(shard, axis, [(i, (i + by) % size) for i in range(size)])]
    all_to_all x1, starting transfers between devices: 10.7 us -> 6.66 us  [on_device(): lax.all_to_all(back, 'expert', 0, 0, axis_index_groups=halves, tiled=True)]
    all_to_all x1, waiting for transfers between devices: 23.6 us -> 19.8 us  [on_device(): lax.all_to_all(back, 'expert', 0, 0, axis_index_groups=halves, tiled=True)]
    unnamed x42 -> x30, local copies, waits for them, and re-layouts: 9.64 us -> 6.27 us
    pallas_call x5 -> x6, Pallas kernels: 8.7 us -> 11.4 us  [call(): pl.pallas_call(kernel, out_shape=jax.ShapeDtypeStruct(shape, dtype), in_s...]
    ppermute x15 -> x16, waiting for transfers between devices: 74.5 us -> 75.1 us  [swapped(): return lax.ppermute(shard, 'expert', [(i, i ^ bits) for i in range(size)])]
  transfers between devices with their start and end apart: 19 -> 20, of which waited for: 11 -> 13; matrix products, arithmetic and copies ran while one was open for 1% -> 1% of each run, Pallas kernels for 1% -> 2%
where the time goes in v2:
time: 218 us; the launch traced here: 217 us
  waiting for transfers between devices  112 us (51%)
  starting transfers between devices  84.2 us (39%)
  Pallas kernels  11.4 us (5%)
  local copies, waits for them, and re-layouts  6.62 us (3%)
    ppermute x16, waiting for transfers between devices, swapped(): return lax.ppermute(shard, 'expert', [(i, i ^ bits) for i in range(size)])  75.1 us
    ppermute x16, starting transfers between devices, swapped(): return lax.ppermute(shard, 'expert', [(i, i ^ bits) for i in range(size)])  52.7 us
    all_to_all x1, waiting for transfers between devices, on_device(): lax.all_to_all(back, 'expert', 0, 0, axis_index_groups=halves, tiled=True)  19.8 us
    ppermute x2, starting transfers between devices, shifted(): lax.ppermute(shard, axis, [(i, (i + by) % size) for i in range(size)])  17.8 us
    ppermute x2, waiting for transfers between devices, shifted(): lax.ppermute(shard, axis, [(i, (i + by) % size) for i in range(size)])  17.4 us
    pallas_call x6, Pallas kernels, call(): pl.pallas_call(kernel, out_shape=jax.ShapeDtypeStruct(shape, dtype), in_s...  11.4 us
    all_to_all x1, starting transfers between devices, on_device(): lax.all_to_all(sent, 'expert', 0, 0, axis_index_groups=columns, tiled=True)  6.95 us
    all_to_all x1, starting transfers between devices, on_device(): lax.all_to_all(back, 'expert', 0, 0, axis_index_groups=halves, tiled=True)  6.66 us
  transfers between devices with their start and end apart: 20, of which 13 were waited for; matrix products, arithmetic and copies ran while one was open for 1% of the time, Pallas kernels for 2%

profile of v2, /device:TPU:7, one launch (start us, length us, event | category | flops | bytes accessed | tf_op | source)
XLA Modules:
  0.0 216.8 jit_solution(13171468255221002664)
XLA Ops:
  0.7 0.6 copy-done.7
  1.3 0.0 copy-done.8
  1.3 1.0 copy-done.2
  2.3 1.0 copy-done.4
  3.3 0.7 copy-done.6
  4.1 1.9 shard_map.113
  5.9 7.0 %all-to-all-start = ((bf16[8,120,512]{2,1,0:T(8,128)(2,1)}), bf16[8,120,512]{2,1,0:T(8,128)(2,1)S(1)}, u32[]{:S(2)}, u32[]{:S(2)}) async-start(bf16[8,120,512]{2,1,0:T(8,128)(2,1)} %shard_map.113), calls=%async_computation | async-start | bytes 1966080 | tf_op jit(solution)/shard_map/all_to_all | solution.py:233
  12.9 4.0 %collective-permute-start = (bf16[3584,128]{1,0:T(8,128)(2,1)S(1)}, bf16[3584,128]{1,0:T(8,128)(2,1)}, u32[]{:S(2)}, u32[]{:S(2)}) collective-permute-start(bf16[3584,128]{1,0:T(8,128)(2,1)S(1)} %bitcast.23), channel_id=1, source_target_pairs={{0,1},{1,0},{2,3},{3,2},{4,5},{5,4},{6,7},{7,6},{8,9},{9,8},{10,11... | collective-permute-start | bytes 2752520 | tf_op jit(solution)/shard_map/ppermute | solution.py:37
  17.0 0.9 select_bitcast_fusion
  17.9 5.9 %collective-permute-start.1 = (bf16[2,128,896]{2,1,0:T(8,128)(2,1)S(1)}, bf16[2,128,896]{2,1,0:T(8,128)(2,1)S(1)}, u32[]{:S(2)}, u32[]{:S(2)}) collective-permute-start(bf16[2,128,896]{2,1,0:T(8,128)(2,1)S(1)} %pad_maximum_fusion.1), channel_id=1, source_target_pairs={{0,2},{1,3},{2,0},{3,1},{4,6},{5,7},{6,4},{7,5},{8,10},{9,11},{10,... | collective-permute-start | bytes 1376264 | tf_op jit(solution)/shard_map/ppermute | solution.py:37
  23.9 21.5 %collective-permute-done.1 = bf16[2,128,896]{2,1,0:T(8,128)(2,1)S(1)} collective-permute-done((bf16[2,128,896]{2,1,0:T(8,128)(2,1)S(1)}, bf16[2,128,896]{2,1,0:T(8,128)(2,1)S(1)}, u32[]{:S(2)}, u32[]{:S(2)}) %collective-permute-start.1) | collective-permute-done | bytes 458784 | tf_op jit(solution)/shard_map/ppermute | solution.py:37
  45.4 1.2 collective-permute-done.refs_3_.refs_5_
  46.6 0.0 all-to-all-done.refs_0_
  46.6 3.0 %collective-permute-start.2 = (bf16[8,120,512]{2,1,0:T(8,128)(2,1)S(1)}, bf16[8,120,512]{2,1,0:T(8,128)(2,1)S(1)}, u32[]{:S(2)}, u32[]{:S(2)}) collective-permute-start(bf16[8,120,512]{2,1,0:T(8,128)(2,1)S(1)} %all-to-all-done.refs_0_), channel_id=1, source_target_pairs={{0,4},{1,5},{2,6},{3,7},{4,0},{5,1},{6,2},{7,3},{8,12},{9,13},{10,... | collective-permute-start | bytes 2949128 | tf_op jit(solution)/shard_map/ppermute | solution.py:37
  49.6 0.0 copy-start.11
  49.6 5.8 %collective-permute-start.4 = (bf16[3584,128]{1,0:T(8,128)(2,1)S(1)}, bf16[3584,128]{1,0:T(8,128)(2,1)S(1)}, u32[]{:S(2)}, u32[]{:S(2)}) collective-permute-start(bf16[3584,128]{1,0:T(8,128)(2,1)S(1)} %bitcast.26), channel_id=1, source_target_pairs={{0,1},{1,0},{2,3},{3,2},{4,5},{5,4},{6,7},{7,6},{8,9},{9,8},{10,11... | collective-permute-start | bytes 2752520 | tf_op jit(solution)/shard_map/ppermute | solution.py:37
  55.5 0.1 pad_maximum_fusion.2
  55.6 2.2 %collective-permute-start.3 = (bf16[2,128,896]{2,1,0:T(8,128)(2,1)S(1)}, bf16[2,128,896]{2,1,0:T(8,128)(2,1)S(1)}, u32[]{:S(2)}, u32[]{:S(2)}) collective-permute-start(bf16[2,128,896]{2,1,0:T(8,128)(2,1)S(1)} %pad_maximum_fusion.2), channel_id=1, source_target_pairs={{0,4},{1,5},{2,6},{3,7},{4,0},{5,1},{6,2},{7,3},{8,12},{9,13},{10,... | collective-permute-start | bytes 1376264 | tf_op jit(solution)/shard_map/ppermute | solution.py:37
  57.9 0.1 fusion
  57.9 3.1 %collective-permute-start.5 = (bf16[4,120,512]{2,1,0:T(8,128)(2,1)S(1)}, bf16[4,120,512]{2,1,0:T(8,128)(2,1)S(1)}, u32[]{:S(2)}, u32[]{:S(2)}) collective-permute-start(bf16[4,120,512]{2,1,0:T(8,128)(2,1)S(1)} %get-tuple-element.25), channel_id=1, source_target_pairs={{0,2},{1,3},{2,0},{3,1},{4,6},{5,7},{6,4},{7,5},{8,10},{9,11},{10,... | collective-permute-start | bytes 1474568 | tf_op jit(solution)/shard_map/ppermute | solution.py:37
  61.1 3.0 %collective-permute-start.6 = (bf16[4,120,512]{2,1,0:T(8,128)(2,1)S(1)}, bf16[4,120,512]{2,1,0:T(8,128)(2,1)S(1)}, u32[]{:S(2)}, u32[]{:S(2)}) collective-permute-start(bf16[4,120,512]{2,1,0:T(8,128)(2,1)S(1)} %get-tuple-element.24), channel_id=1, source_target_pairs={{0,2},{1,3},{2,0},{3,1},{4,6},{5,7},{6,4},{7,5},{8,10},{9,11},{10,... | collective-permute-start | bytes 1474568 | tf_op jit(solution)/shard_map/ppermute | solution.py:37
  64.1 15.9 %collective-permute-done.3 = bf16[2,128,896]{2,1,0:T(8,128)(2,1)S(1)} collective-permute-done((bf16[2,128,896]{2,1,0:T(8,128)(2,1)S(1)}, bf16[2,128,896]{2,1,0:T(8,128)(2,1)S(1)}, u32[]{:S(2)}, u32[]{:S(2)}) %collective-permute-start.3) | collective-permute-done | bytes 458784 | tf_op jit(solution)/shard_map/ppermute | solution.py:37
  80.0 0.0 collective-permute-done.2.refs_1_
  80.0 0.0 copy-start.10
  80.1 7.9 %collective-permute-done.4.refs_5_.refs_7_ = bf16[3584,128]{1,0:T(8,128)(2,1)S(1)} collective-permute-done((bf16[3584,128]{1,0:T(8,128)(2,1)S(1)}, bf16[3584,128]{1,0:T(8,128)(2,1)S(1)}, u32[]{:S(2)}, u32[]{:S(2)}) %collective-permute-start.4) | collective-permute-done | bytes 917536 | tf_op jit(solution)/shard_map/ppermute | solution.py:37
  87.9 2.4 %shard_map.114.refs_0_ = bf16[272,256]{1,0:T(8,128)(2,1)S(1)} custom-call(bf16[8,120,512]{2,1,0:T(8,128)(2,1)S(1)} %all-to-all-done.refs_0_, bf16[8,120,512]{2,1,0:T(8,128)(2,1)S(1)} %collective-permute-done.2.refs_1_, bf16[3584,128]{1,0:T(8,128)(2,1)S(1)} %bitcast.24, bf16[3584,128]{1,0:T(8,128)(2,1)} %collective-permute-done.refs_3_.refs_5_, ...), custom_call_target="tpu_custom_call" | custom-call | tf_op jit(solution)/shard_map/pallas_call | solution.py:164
  90.4 0.1 pad_maximum_fusion.refs_8_
  90.5 1.9 collective-permute-start.15
  92.4 10.4 %collective-permute-done.6.refs_1_ = bf16[4,120,512]{2,1,0:T(8,128)(2,1)S(1)} collective-permute-done((bf16[4,120,512]{2,1,0:T(8,128)(2,1)S(1)}, bf16[4,120,512]{2,1,0:T(8,128)(2,1)S(1)}, u32[]{:S(2)}, u32[]{:S(2)}) %collective-permute-start.6) | collective-permute-done | bytes 491552 | tf_op jit(solution)/shard_map/ppermute | solution.py:37
  102.8 2.7 %collective-permute-start.8 = (bf16[4,120,512]{2,1,0:T(8,128)(2,1)S(1)}, bf16[4,120,512]{2,1,0:T(8,128)(2,1)S(1)}, u32[]{:S(2)}, u32[]{:S(2)}) collective-permute-start(bf16[4,120,512]{2,1,0:T(8,128)(2,1)S(1)} %collective-permute-done.6.refs_1_), channel_id=1, source_target_pairs={{0,4},{1,5},{2,6},{3,7},{4,0},{5,1},{6,2},{7,3},{8,12},{9,13},{10,... | collective-permute-start | bytes 1474568 | tf_op jit(solution)/shard_map/ppermute | solution.py:37
  105.5 0.0 collective-permute-done.5.refs_0_
  105.5 2.6 %collective-permute-start.7 = (bf16[4,120,512]{2,1,0:T(8,128)(2,1)S(1)}, bf16[4,120,512]{2,1,0:T(8,128)(2,1)S(1)}, u32[]{:S(2)}, u32[]{:S(2)}) collective-permute-start(bf16[4,120,512]{2,1,0:T(8,128)(2,1)S(1)} %collective-permute-done.5.refs_0_), channel_id=1, source_target_pairs={{0,4},{1,5},{2,6},{3,7},{4,0},{5,1},{6,2},{7,3},{8,12},{9,13},{10,... | collective-permute-start | bytes 1474568 | tf_op jit(solution)/shard_map/ppermute | solution.py:37
  108.1 2.7 %collective-permute-start.9 = (bf16[272,256]{1,0:T(8,128)(2,1)S(1)}, bf16[272,256]{1,0:T(8,128)(2,1)S(1)}, u32[]{:S(2)}, u32[]{:S(2)}) collective-permute-start(bf16[272,256]{1,0:T(8,128)(2,1)S(1)} %shard_map.114.refs_0_), channel_id=1, source_target_pairs={{0,4},{1,5},{2,6},{3,7},{4,0},{5,1},{6,2},{7,3},{8,12},{9,13},{10,... | collective-permute-start | bytes 417800 | tf_op jit(solution)/shard_map/ppermute | solution.py:37
  110.8 1.9 collective-permute-start.10
  112.7 1.4 collective-permute-done.8.refs_3_
  114.2 3.2 %collective-permute-start.11 = (bf16[272,256]{1,0:T(8,128)(2,1)S(1)}, bf16[272,256]{1,0:T(8,128)(2,1)S(1)}, u32[]{:S(2)}, u32[]{:S(2)}) collective-permute-start(bf16[272,256]{1,0:T(8,128)(2,1)S(1)} %shard_map.114.refs_0_), channel_id=1, source_target_pairs={{0,6},{1,7},{2,4},{3,5},{4,2},{5,3},{6,0},{7,1},{8,14},{9,15},{10,... | collective-permute-start | bytes 417800 | tf_op jit(solution)/shard_map/ppermute | solution.py:37
  117.4 10.2 %collective-permute-done.9.refs_2_ = bf16[272,256]{1,0:T(8,128)(2,1)S(1)} collective-permute-done((bf16[272,256]{1,0:T(8,128)(2,1)S(1)}, bf16[272,256]{1,0:T(8,128)(2,1)S(1)}, u32[]{:S(2)}, u32[]{:S(2)}) %collective-permute-start.9) | collective-permute-done | bytes 139296 | tf_op jit(solution)/shard_map/ppermute | solution.py:37
  127.6 0.0 collective-permute-done.10.refs_4_
  127.6 1.7 collective-permute-done.11.refs_6_
  129.3 0.0 collective-permute-done.7.refs_2_
  129.3 2.4 %shard_map.115.refs_1_ = bf16[272,256]{1,0:T(8,128)(2,1)S(1)} custom-call(bf16[4,120,512]{2,1,0:T(8,128)(2,1)S(1)} %collective-permute-done.5.refs_0_, bf16[4,120,512]{2,1,0:T(8,128)(2,1)S(1)} %collective-permute-done.6.refs_1_, bf16[4,120,512]{2,1,0:T(8,128)(2,1)S(1)} %collective-permute-done.7.refs_2_, ...), custom_call_target="tpu_custom_call" | custom-call | tf_op jit(solution)/shard_map/pallas_call | solution.py:164
  131.7 2.4 %collective-permute-start.12 = (bf16[272,256]{1,0:T(8,128)(2,1)S(1)}, bf16[272,256]{1,0:T(8,128)(2,1)S(1)}, u32[]{:S(2)}, u32[]{:S(2)}) collective-permute-start(bf16[272,256]{1,0:T(8,128)(2,1)S(1)} %shard_map.115.refs_1_), channel_id=1, source_target_pairs={{0,4},{1,5},{2,6},{3,7},{4,0},{5,1},{6,2},{7,3},{8,12},{9,13},{10,... | collective-permute-start | bytes 417800 | tf_op jit(solution)/shard_map/ppermute | solution.py:37
  134.2 5.1 %collective-permute-start.13 = (bf16[272,256]{1,0:T(8,128)(2,1)S(1)}, bf16[272,256]{1,0:T(8,128)(2,1)S(1)}, u32[]{:S(2)}, u32[]{:S(2)}) collective-permute-start(bf16[272,256]{1,0:T(8,128)(2,1)S(1)} %shard_map.115.refs_1_), channel_id=1, source_target_pairs={{0,2},{1,3},{2,0},{3,1},{4,6},{5,7},{6,4},{7,5},{8,10},{9,11},{10,... | collective-permute-start | bytes 417800 | tf_op jit(solution)/shard_map/ppermute | solution.py:37
  139.3 2.9 %collective-permute-start.14 = (bf16[272,256]{1,0:T(8,128)(2,1)S(1)}, bf16[272,256]{1,0:T(8,128)(2,1)S(1)}, u32[]{:S(2)}, u32[]{:S(2)}) collective-permute-start(bf16[272,256]{1,0:T(8,128)(2,1)S(1)} %shard_map.115.refs_1_), channel_id=1, source_target_pairs={{0,6},{1,7},{2,4},{3,5},{4,2},{5,3},{6,0},{7,1},{8,14},{9,15},{10,... | collective-permute-start | bytes 417800 | tf_op jit(solution)/shard_map/ppermute | solution.py:37
  142.2 0.1 pad_add_fusion.places
  142.3 0.0 collective-permute-done.12.refs_3_
  142.3 0.9 collective-permute-done.13.refs_5_
  143.2 4.1 %collective-permute-done.14.refs_7_ = bf16[272,256]{1,0:T(8,128)(2,1)S(1)} collective-permute-done((bf16[272,256]{1,0:T(8,128)(2,1)S(1)}, bf16[272,256]{1,0:T(8,128)(2,1)S(1)}, u32[]{:S(2)}, u32[]{:S(2)}) %collective-permute-start.14) | collective-permute-done | bytes 139296 | tf_op jit(solution)/shard_map/ppermute | solution.py:37
  147.3 3.6 %shard_map.116 = bf16[16,2,120,128]{3,2,1,0:T(8,128)(2,1)} custom-call(s32[4]{0:T(128)S(1)} %pad_add_fusion.places, bf16[272,256]{1,0:T(8,128)(2,1)S(1)} %shard_map.114.refs_0_, bf16[272,256]{1,0:T(8,128)(2,1)S(1)} %shard_map.115.refs_1_, bf16[272,256]{1,0:T(8,128)(2,1)S(1)} %collective-permute-done.9.refs_2_, ...), custom_call_target="tpu_custom_call" | custom-call | tf_op jit(solution)/shard_map/pallas_call | solution.py:164
  150.9 6.7 %all-to-all-start.1 = ((bf16[16,2,120,128]{3,2,1,0:T(8,128)(2,1)}), bf16[16,2,120,128]{3,2,1,0:T(8,128)(2,1)S(1)}, u32[]{:S(2)}, u32[]{:S(2)}) async-start(bf16[16,2,120,128]{3,2,1,0:T(8,128)(2,1)} %shard_map.116), calls=%async_computation.1 | async-start | bytes 1966080 | tf_op jit(solution)/shard_map/all_to_all | solution.py:268
  157.6 0.0 copy-start.12
  157.6 0.6 copy-done.12
  158.2 0.1 copy.12.gate_ref
  158.3 0.7 copy-done.13
  159.0 0.1 copy.13.gate_ref
  159.1 19.8 %all-to-all-done.1.got_ref = bf16[16,2,120,128]{3,2,1,0:T(8,128)(2,1)S(1)} async-done(((bf16[16,2,120,128]{3,2,1,0:T(8,128)(2,1)}), bf16[16,2,120,128]{3,2,1,0:T(8,128)(2,1)S(1)}, u32[]{:S(2)}, u32[]{:S(2)}) %all-to-all-start.1) | async-done | bytes 983072 | tf_op jit(solution)/shard_map/all_to_all | solution.py:268
  178.9 0.6 shard_map.117
  179.5 15.9 %collective-permute-start.16 = (bf16[1,64,3584]{2,1,0:T(8,128)(2,1)S(1)}, bf16[1,64,3584]{2,1,0:T(8,128)(2,1)S(1)}, u32[]{:S(2)}, u32[]{:S(2)}) collective-permute-start(bf16[1,64,3584]{2,1,0:T(8,128)(2,1)S(1)} %bitcast.33), channel_id=1, source_target_pairs={{0,32},{32,64},{64,96},{96,128},{128,160},{160,192},{192,224},{224... | collective-permute-start | bytes 1376264 | tf_op jit(solution)/shard_map/ppermute | solution.py:32
  195.4 0.6 shard_map.118
  196.0 1.9 collective-permute-start.17
  197.9 6.3 %collective-permute-done.16 = bf16[1,64,3584]{2,1,0:T(8,128)(2,1)S(1)} collective-permute-done((bf16[1,64,3584]{2,1,0:T(8,128)(2,1)S(1)}, bf16[1,64,3584]{2,1,0:T(8,128)(2,1)S(1)}, u32[]{:S(2)}, u32[]{:S(2)}) %collective-permute-start.16) | collective-permute-done | bytes 458784 | tf_op jit(solution)/shard_map/ppermute | solution.py:32
  204.2 11.1 %collective-permute-done.17 = bf16[1,64,3584]{2,1,0:T(8,128)(2,1)S(1)} collective-permute-done((bf16[1,64,3584]{2,1,0:T(8,128)(2,1)S(1)}, bf16[1,64,3584]{2,1,0:T(8,128)(2,1)S(1)}, u32[]{:S(2)}, u32[]{:S(2)}) %collective-permute-start.17) | collective-permute-done | bytes 458784 | tf_op jit(solution)/shard_map/ppermute | solution.py:32
  215.3 0.8 copy.16
  216.1 0.8 copy.17
  (22 shorter events, 0.2 us)
Async XLA Ops:
  0.6 0.7 copy-start.7
  0.6 0.7 copy-start.8
  1.3 1.0 copy-start.2
  2.3 1.0 copy-start.4
  3.3 0.7 copy-start.6
  5.9 7.0 %copy-start = (bf16[1,3584,128]{2,1,0:T(8,128)(2,1)S(1)}, bf16[1,3584,128]{2,1,0:T(8,128)(2,1)}, u32[]{:S(2)}) copy-start(bf16[1,3584,128]{2,1,0:T(8,128)(2,1)} %param.17) | copy-start | bytes 2752516
  5.9 11.0 %copy-start.9 = (bf16[1,128,3584]{2,1,0:T(8,128)(2,1)S(1)}, bf16[1,128,3584]{2,1,0:T(8,128)(2,1)}, u32[]{:S(2)}) copy-start(bf16[1,128,3584]{2,1,0:T(8,128)(2,1)} %param.19) | copy-start | bytes 2752516
  5.9 40.7 %all-to-all-start = ((bf16[8,120,512]{2,1,0:T(8,128)(2,1)}), bf16[8,120,512]{2,1,0:T(8,128)(2,1)S(1)}, u32[]{:S(2)}, u32[]{:S(2)}) async-start(bf16[8,120,512]{2,1,0:T(8,128)(2,1)} %shard_map.113), calls=%async_computation | async-start | bytes 1966080 | tf_op jit(solution)/shard_map/all_to_all | solution.py:233
  12.9 33.7 %collective-permute-start = (bf16[3584,128]{1,0:T(8,128)(2,1)S(1)}, bf16[3584,128]{1,0:T(8,128)(2,1)}, u32[]{:S(2)}, u32[]{:S(2)}) collective-permute-start(bf16[3584,128]{1,0:T(8,128)(2,1)S(1)} %bitcast.23), channel_id=1, source_target_pairs={{0,1},{1,0},{2,3},{3,2},{4,5},{5,4},{6,7},{7,6},{8,9},{9,8},{10,11... | collective-permute-start | bytes 2752520 | tf_op jit(solution)/shard_map/ppermute | solution.py:37
  17.9 31.7 %copy-start.1 = (bf16[1,3584,128]{2,1,0:T(8,128)(2,1)S(1)}, bf16[1,3584,128]{2,1,0:T(8,128)(2,1)}, u32[]{:S(2)}) copy-start(bf16[1,3584,128]{2,1,0:T(8,128)(2,1)} %param.18) | copy-start | bytes 2752516
  17.9 27.5 %collective-permute-start.1 = (bf16[2,128,896]{2,1,0:T(8,128)(2,1)S(1)}, bf16[2,128,896]{2,1,0:T(8,128)(2,1)S(1)}, u32[]{:S(2)}, u32[]{:S(2)}) collective-permute-start(bf16[2,128,896]{2,1,0:T(8,128)(2,1)S(1)} %pad_maximum_fusion.1), channel_id=1, source_target_pairs={{0,2},{1,3},{2,0},{3,1},{4,6},{5,7},{6,4},{7,5},{8,10},{9,11},{10,... | collective-permute-start | bytes 1376264 | tf_op jit(solution)/shard_map/ppermute | solution.py:37
  46.6 33.4 %collective-permute-start.2 = (bf16[8,120,512]{2,1,0:T(8,128)(2,1)S(1)}, bf16[8,120,512]{2,1,0:T(8,128)(2,1)S(1)}, u32[]{:S(2)}, u32[]{:S(2)}) collective-permute-start(bf16[8,120,512]{2,1,0:T(8,128)(2,1)S(1)} %all-to-all-done.refs_0_), channel_id=1, source_target_pairs={{0,4},{1,5},{2,6},{3,7},{4,0},{5,1},{6,2},{7,3},{8,12},{9,13},{10,... | collective-permute-start | bytes 2949128 | tf_op jit(solution)/shard_map/ppermute | solution.py:37
  49.6 5.9 %copy-start.11 = (bf16[1,128,896]{2,1,0:T(8,128)(2,1)S(1)}, bf16[1,128,896]{2,1,0:T(8,128)(2,1)}, u32[]{:S(2)}) copy-start(bf16[1,128,896]{2,1,0:T(8,128)(2,1)} %get-tuple-element.28) | copy-start | bytes 688132
  49.6 38.3 %collective-permute-start.4 = (bf16[3584,128]{1,0:T(8,128)(2,1)S(1)}, bf16[3584,128]{1,0:T(8,128)(2,1)S(1)}, u32[]{:S(2)}, u32[]{:S(2)}) collective-permute-start(bf16[3584,128]{1,0:T(8,128)(2,1)S(1)} %bitcast.26), channel_id=1, source_target_pairs={{0,1},{1,0},{2,3},{3,2},{4,5},{5,4},{6,7},{7,6},{8,9},{9,8},{10,11... | collective-permute-start | bytes 2752520 | tf_op jit(solution)/shard_map/ppermute | solution.py:37
  55.6 24.4 %collective-permute-start.3 = (bf16[2,128,896]{2,1,0:T(8,128)(2,1)S(1)}, bf16[2,128,896]{2,1,0:T(8,128)(2,1)S(1)}, u32[]{:S(2)}, u32[]{:S(2)}) collective-permute-start(bf16[2,128,896]{2,1,0:T(8,128)(2,1)S(1)} %pad_maximum_fusion.2), channel_id=1, source_target_pairs={{0,4},{1,5},{2,6},{3,7},{4,0},{5,1},{6,2},{7,3},{8,12},{9,13},{10,... | collective-permute-start | bytes 1376264 | tf_op jit(solution)/shard_map/ppermute | solution.py:37
  57.9 47.6 %collective-permute-start.5 = (bf16[4,120,512]{2,1,0:T(8,128)(2,1)S(1)}, bf16[4,120,512]{2,1,0:T(8,128)(2,1)S(1)}, u32[]{:S(2)}, u32[]{:S(2)}) collective-permute-start(bf16[4,120,512]{2,1,0:T(8,128)(2,1)S(1)} %get-tuple-element.25), channel_id=1, source_target_pairs={{0,2},{1,3},{2,0},{3,1},{4,6},{5,7},{6,4},{7,5},{8,10},{9,11},{10,... | collective-permute-start | bytes 1474568 | tf_op jit(solution)/shard_map/ppermute | solution.py:37
  61.1 41.7 %collective-permute-start.6 = (bf16[4,120,512]{2,1,0:T(8,128)(2,1)S(1)}, bf16[4,120,512]{2,1,0:T(8,128)(2,1)S(1)}, u32[]{:S(2)}, u32[]{:S(2)}) collective-permute-start(bf16[4,120,512]{2,1,0:T(8,128)(2,1)S(1)} %get-tuple-element.24), channel_id=1, source_target_pairs={{0,2},{1,3},{2,0},{3,1},{4,6},{5,7},{6,4},{7,5},{8,10},{9,11},{10,... | collective-permute-start | bytes 1474568 | tf_op jit(solution)/shard_map/ppermute | solution.py:37
  80.0 10.3 %copy-start.10 = (bf16[1,128,896]{2,1,0:T(8,128)(2,1)S(1)}, bf16[1,128,896]{2,1,0:T(8,128)(2,1)}, u32[]{:S(2)}) copy-start(bf16[1,128,896]{2,1,0:T(8,128)(2,1)} %get-tuple-element.26) | copy-start | bytes 688132
  90.5 56.8 %collective-permute-start.15 = (bf16[4,128,896]{2,1,0:T(8,128)(2,1)S(1)}, bf16[4,128,896]{2,1,0:T(8,128)(2,1)}, u32[]{:S(2)}, u32[]{:S(2)}) collective-permute-start(bf16[4,128,896]{2,1,0:T(8,128)(2,1)S(1)} %pad_maximum_fusion.refs_8_), channel_id=1, source_target_pairs={{0,1},{1,0},{2,3},{3,2},{4,5},{5,4},{6,7},{7,6},{8,9},{9,8},{10,11... | collective-permute-start | bytes 2752520 | tf_op jit(solution)/shard_map/ppermute | solution.py:37
  102.8 11.4 %collective-permute-start.8 = (bf16[4,120,512]{2,1,0:T(8,128)(2,1)S(1)}, bf16[4,120,512]{2,1,0:T(8,128)(2,1)S(1)}, u32[]{:S(2)}, u32[]{:S(2)}) collective-permute-start(bf16[4,120,512]{2,1,0:T(8,128)(2,1)S(1)} %collective-permute-done.6.refs_1_), channel_id=1, source_target_pairs={{0,4},{1,5},{2,6},{3,7},{4,0},{5,1},{6,2},{7,3},{8,12},{9,13},{10,... | collective-permute-start | bytes 1474568 | tf_op jit(solution)/shard_map/ppermute | solution.py:37
  105.5 23.8 %collective-permute-start.7 = (bf16[4,120,512]{2,1,0:T(8,128)(2,1)S(1)}, bf16[4,120,512]{2,1,0:T(8,128)(2,1)S(1)}, u32[]{:S(2)}, u32[]{:S(2)}) collective-permute-start(bf16[4,120,512]{2,1,0:T(8,128)(2,1)S(1)} %collective-permute-done.5.refs_0_), channel_id=1, source_target_pairs={{0,4},{1,5},{2,6},{3,7},{4,0},{5,1},{6,2},{7,3},{8,12},{9,13},{10,... | collective-permute-start | bytes 1474568 | tf_op jit(solution)/shard_map/ppermute | solution.py:37
  108.1 19.5 %collective-permute-start.9 = (bf16[272,256]{1,0:T(8,128)(2,1)S(1)}, bf16[272,256]{1,0:T(8,128)(2,1)S(1)}, u32[]{:S(2)}, u32[]{:S(2)}) collective-permute-start(bf16[272,256]{1,0:T(8,128)(2,1)S(1)} %shard_map.114.refs_0_), channel_id=1, source_target_pairs={{0,4},{1,5},{2,6},{3,7},{4,0},{5,1},{6,2},{7,3},{8,12},{9,13},{10,... | collective-permute-start | bytes 417800 | tf_op jit(solution)/shard_map/ppermute | solution.py:37
  110.8 16.8 %collective-permute-start.10 = (bf16[272,256]{1,0:T(8,128)(2,1)S(1)}, bf16[272,256]{1,0:T(8,128)(2,1)S(1)}, u32[]{:S(2)}, u32[]{:S(2)}) collective-permute-start(bf16[272,256]{1,0:T(8,128)(2,1)S(1)} %shard_map.114.refs_0_), channel_id=1, source_target_pairs={{0,2},{1,3},{2,0},{3,1},{4,6},{5,7},{6,4},{7,5},{8,10},{9,11},{10,... | collective-permute-start | bytes 417800 | tf_op jit(solution)/shard_map/ppermute | solution.py:37
  114.2 15.1 %collective-permute-start.11 = (bf16[272,256]{1,0:T(8,128)(2,1)S(1)}, bf16[272,256]{1,0:T(8,128)(2,1)S(1)}, u32[]{:S(2)}, u32[]{:S(2)}) collective-permute-start(bf16[272,256]{1,0:T(8,128)(2,1)S(1)} %shard_map.114.refs_0_), channel_id=1, source_target_pairs={{0,6},{1,7},{2,4},{3,5},{4,2},{5,3},{6,0},{7,1},{8,14},{9,15},{10,... | collective-permute-start | bytes 417800 | tf_op jit(solution)/shard_map/ppermute | solution.py:37
  131.7 10.6 %collective-permute-start.12 = (bf16[272,256]{1,0:T(8,128)(2,1)S(1)}, bf16[272,256]{1,0:T(8,128)(2,1)S(1)}, u32[]{:S(2)}, u32[]{:S(2)}) collective-permute-start(bf16[272,256]{1,0:T(8,128)(2,1)S(1)} %shard_map.115.refs_1_), channel_id=1, source_target_pairs={{0,4},{1,5},{2,6},{3,7},{4,0},{5,1},{6,2},{7,3},{8,12},{9,13},{10,... | collective-permute-start | bytes 417800 | tf_op jit(solution)/shard_map/ppermute | solution.py:37
  134.2 9.0 %collective-permute-start.13 = (bf16[272,256]{1,0:T(8,128)(2,1)S(1)}, bf16[272,256]{1,0:T(8,128)(2,1)S(1)}, u32[]{:S(2)}, u32[]{:S(2)}) collective-permute-start(bf16[272,256]{1,0:T(8,128)(2,1)S(1)} %shard_map.115.refs_1_), channel_id=1, source_target_pairs={{0,2},{1,3},{2,0},{3,1},{4,6},{5,7},{6,4},{7,5},{8,10},{9,11},{10,... | collective-permute-start | bytes 417800 | tf_op jit(solution)/shard_map/ppermute | solution.py:37
  139.3 8.0 %collective-permute-start.14 = (bf16[272,256]{1,0:T(8,128)(2,1)S(1)}, bf16[272,256]{1,0:T(8,128)(2,1)S(1)}, u32[]{:S(2)}, u32[]{:S(2)}) collective-permute-start(bf16[272,256]{1,0:T(8,128)(2,1)S(1)} %shard_map.115.refs_1_), channel_id=1, source_target_pairs={{0,6},{1,7},{2,4},{3,5},{4,2},{5,3},{6,0},{7,1},{8,14},{9,15},{10,... | collective-permute-start | bytes 417800 | tf_op jit(solution)/shard_map/ppermute | solution.py:37
  150.9 28.0 %copy-start.3 = (bf16[1,64,3584]{2,1,0:T(8,128)(2,1)S(1)}, bf16[1,64,3584]{2,1,0:T(8,128)(2,1)}, u32[]{:S(2)}) copy-start(bf16[1,64,3584]{2,1,0:T(8,128)(2,1)} %param.10) | copy-start | bytes 1376260
  150.9 28.0 %all-to-all-start.1 = ((bf16[16,2,120,128]{3,2,1,0:T(8,128)(2,1)}), bf16[16,2,120,128]{3,2,1,0:T(8,128)(2,1)S(1)}, u32[]{:S(2)}, u32[]{:S(2)}) async-start(bf16[16,2,120,128]{3,2,1,0:T(8,128)(2,1)} %shard_map.116), calls=%async_computation.1 | async-start | bytes 1966080 | tf_op jit(solution)/shard_map/all_to_all | solution.py:268
  157.6 0.7 copy-start.12
  158.3 0.7 copy-start.13
  159.1 36.3 %copy-start.5 = (bf16[1,64,3584]{2,1,0:T(8,128)(2,1)S(1)}, bf16[1,64,3584]{2,1,0:T(8,128)(2,1)}, u32[]{:S(2)}) copy-start(bf16[1,64,3584]{2,1,0:T(8,128)(2,1)} %param.11) | copy-start | bytes 1376260
  179.5 24.8 %collective-permute-start.16 = (bf16[1,64,3584]{2,1,0:T(8,128)(2,1)S(1)}, bf16[1,64,3584]{2,1,0:T(8,128)(2,1)S(1)}, u32[]{:S(2)}, u32[]{:S(2)}) collective-permute-start(bf16[1,64,3584]{2,1,0:T(8,128)(2,1)S(1)} %bitcast.33), channel_id=1, source_target_pairs={{0,32},{32,64},{64,96},{96,128},{128,160},{160,192},{192,224},{224... | collective-permute-start | bytes 1376264 | tf_op jit(solution)/shard_map/ppermute | solution.py:32
  196.0 19.3 %collective-permute-start.17 = (bf16[1,64,3584]{2,1,0:T(8,128)(2,1)S(1)}, bf16[1,64,3584]{2,1,0:T(8,128)(2,1)S(1)}, u32[]{:S(2)}, u32[]{:S(2)}) collective-permute-start(bf16[1,64,3584]{2,1,0:T(8,128)(2,1)S(1)} %bitcast.34), channel_id=1, source_target_pairs={{0,480},{32,0},{64,32},{96,64},{128,96},{160,128},{192,160},{224,1... | collective-permute-start | bytes 1376264 | tf_op jit(solution)/shard_map/ppermute | solution.py:32

commit v3 on v2

--- a/solution.py
+++ b/solution.py
@@ -17,6 +17,7 @@
 TOK = 64
 WIDE = 512
 GROUPS = D // WIDE
+EARLY = 4 * WIDE
 PART = D // RUN
 CUT = 128
 CUTS = PART // CUT
@@ -75,7 +76,7 @@
 
 
 def hidden_kernel(*refs):
-    *parts, ga, gb, ua, ub, out_ref, acc_ref, last_ref = refs
+    *parts, ga, gb_low, gb_high, ua, ub, out_ref, acc_ref, last_ref = refs
     at = 0
     for x in parts:
         last_ref[at : at + x.shape[0]] = x[:, GROUPS * MAIN :, :].astype(F32)
@@ -90,8 +91,12 @@
         )
         rows = jnp.concatenate([rows, last_ref[:, g, :].astype(BF16)], axis=0)
         here = pl.ds(g * WIDE, WIDE)
-        for n, (g_w, u_w) in enumerate(((ga, ua), (gb, ub))):
-            w = jnp.concatenate([g_w[here, :], u_w[here, :]], axis=1)
+        if g * WIDE < EARLY:
+            gb = gb_low[here, :]
+        else:
+            gb = gb_high[pl.ds(g * WIDE - EARLY, WIDE), :]
+        for n, (g_w, u_w) in enumerate(((ga[here, :], ua[here, :]), (gb, ub[here, :]))):
+            w = jnp.concatenate([g_w, u_w], axis=1)
             got = jnp.dot(rows, w, preferred_element_type=F32)
             cols = slice(n * 256, (n + 1) * 256)
             if g == 0:
@@ -202,7 +207,7 @@
     lead_e = lead_experts[0, :, 0][None, :]
     tail_e = tail_experts[0, :, 0][None, :]
     gate_w, up_w, down_w = gate_proj[0], up_proj[0], down_proj[0]
-    gate_b, up_b = swapped(gate_w, NEAR), swapped(up_w, NEAR)
+    gate_low = swapped(gate_w[:EARLY], NEAR)
 
     cuts = [down_w[:, n * PART : (n + 1) * PART] for n in range(RUN)]
     mine = 2 * twin + far
@@ -232,21 +237,23 @@
     columns = [[y * RUN + r for y in range(senders)] for r in range(RUN)]
     own = lax.all_to_all(sent, "expert", 0, 0, axis_index_groups=columns, tiled=True)
     step = lax.optimization_barrier
-    own, gate_b, from_far = step((own, gate_b, from_far))
-    half = senders // 2
-    near_rows, far_rows = swapped(own[:half], TEAM[2]), swapped(own[half:], TEAM[2])
+    own, gate_low, from_far, rest, up_w = step(
+        (own, gate_low, from_far, gate_w[EARLY:], up_w)
+    )
+    gate_high, up_b = swapped(rest, NEAR), swapped(up_w, NEAR)
+    far_rows = swapped(own, TEAM[2])
     beside = swapped(own, TEAM[1])
     from_twin = swapped(jnp.stack([parts[1], from_far[1]]), TEAM[1])
-    beside, from_twin = step((beside, from_twin))
-    weights = (gate_w, gate_b, up_w, up_b)
+    beside, from_twin, up_b, gate_high = step((beside, from_twin, up_b, gate_high))
+    weights = (gate_w, gate_low, gate_high, up_w, up_b)
     early = hidden_of((own, beside), weights)
     down_a = jnp.stack([parts[0], from_twin[0], from_far[0], from_twin[1]])
-    early, down_a = step((early, down_a))
+    far_rows, down_a = step((far_rows, down_a))
     down_b = swapped(down_a, NEAR)
     early_sent = [swapped(early, TEAM[k]) for k in range(1, RUN)]
-    near_last, far_last = swapped(near_rows, TEAM[1]), swapped(far_rows, TEAM[1])
+    far_last = swapped(far_rows, TEAM[1])
     far_last, early_sent = step((far_last, early_sent))
-    late = hidden_of((near_rows, far_rows, near_last, far_last), weights)
+    late = hidden_of((far_rows, far_last), weights)
     hs = [early, late]
     for k in range(1, RUN):
         hs += [early_sent[k - 1], swapped(late, TEAM[k])]

time: 218 us -> 216 us (level)
  local copies, waits for them, and re-layouts: 6.62 us -> 9.96 us
  waiting for transfers between devices: 112 us -> 109 us
  Pallas kernels: 11.4 us -> 9.02 us
    pallas_call x6, Pallas kernels: 11.4 us -> 9.02 us  [call(): pl.pallas_call(kernel, out_shape=jax.ShapeDtypeStruct(shape, dtype), in_s...]
    ppermute x2, starting transfers between devices: 17.8 us -> 20.2 us  [shifted(): lax.ppermute(shard, axis, [(i, (i + by) % size) for i in range(size)])]
    ppermute x16 -> x15, starting transfers between devices: 52.7 us -> 50.4 us  [swapped(): return lax.ppermute(shard, 'expert', [(i, i ^ bits) for i in range(size)])]
    ppermute x16 -> x15, waiting for transfers between devices: 75.1 us -> 73.5 us  [swapped(): return lax.ppermute(shard, 'expert', [(i, i ^ bits) for i in range(size)])]
    unnamed x30 -> x36, local copies, waits for them, and re-layouts: 6.27 us -> 7.05 us
  transfers between devices with their start and end apart: 20 -> 19, of which waited for: 13 -> 10; matrix products, arithmetic and copies ran while one was open for 1% -> 2% of each run, Pallas kernels for 2% -> 1%
where the time goes in v3:
time: 216 us; the launch traced here: 215 us
  waiting for transfers between devices  109 us (50%)
  starting transfers between devices  84.5 us (39%)
  local copies, waits for them, and re-layouts  9.96 us (5%)
  Pallas kernels  9.02 us (4%)
    ppermute x15, waiting for transfers between devices, swapped(): return lax.ppermute(shard, 'expert', [(i, i ^ bits) for i in range(size)])  73.5 us
    ppermute x15, starting transfers between devices, swapped(): return lax.ppermute(shard, 'expert', [(i, i ^ bits) for i in range(size)])  50.4 us
    ppermute x2, starting transfers between devices, shifted(): lax.ppermute(shard, axis, [(i, (i + by) % size) for i in range(size)])  20.2 us
    ppermute x2, waiting for transfers between devices, shifted(): lax.ppermute(shard, axis, [(i, (i + by) % size) for i in range(size)])  17.7 us
    all_to_all x1, waiting for transfers between devices, on_device(): lax.all_to_all(back, 'expert', 0, 0, axis_index_groups=halves, tiled=True)  17.6 us
    pallas_call x6, Pallas kernels, call(): pl.pallas_call(kernel, out_shape=jax.ShapeDtypeStruct(shape, dtype), in_s...  9.02 us
    unnamed x36, local copies, waits for them, and re-layouts  7.05 us
    all_to_all x1, starting transfers between devices, on_device(): lax.all_to_all(back, 'expert', 0, 0, axis_index_groups=halves, tiled=True)  6.98 us
  transfers between devices with their start and end apart: 19, of which 10 were waited for; matrix products, arithmetic and copies ran while one was open for 2% of the time, Pallas kernels for 1%

profile of v3, /device:TPU:7, one launch (start us, length us, event | category | flops | bytes accessed | tf_op | source)
XLA Modules:
  0.0 214.6 jit_solution(15123265951639141121)
XLA Ops:
  0.7 0.6 copy-done.8
  1.3 0.0 copy-done.9
  1.3 1.0 copy-done.3
  2.3 1.0 copy-done.5
  3.3 0.7 copy-done.7
  4.1 1.9 shard_map.113
  5.9 7.0 %all-to-all-start = ((bf16[8,120,512]{2,1,0:T(8,128)(2,1)}), bf16[8,120,512]{2,1,0:T(8,128)(2,1)S(1)}, u32[]{:S(2)}, u32[]{:S(2)}) async-start(bf16[8,120,512]{2,1,0:T(8,128)(2,1)} %shard_map.113), calls=%async_computation | async-start | bytes 1966080 | tf_op jit(solution)/shard_map/all_to_all | solution.py:238
  12.9 0.0 copy-start.10
  12.9 0.8 slice_bitcast_fusion
  13.7 4.0 %collective-permute-start = (bf16[2048,128]{1,0:T(8,128)(2,1)}, bf16[2048,128]{1,0:T(8,128)(2,1)S(1)}, u32[]{:S(2)}, u32[]{:S(2)}) collective-permute-start(bf16[2048,128]{1,0:T(8,128)(2,1)} %slice_bitcast_fusion), channel_id=1, source_target_pairs={{0,1},{1,0},{2,3},{3,2},{4,5},{5,4},{6,7},{7,6},{8,9},{9,8},{10,11... | collective-permute-start | bytes 1572872 | tf_op jit(solution)/shard_map/ppermute | solution.py:38
  17.8 0.9 select_bitcast_fusion
  18.8 5.9 %collective-permute-start.1 = (bf16[2,128,896]{2,1,0:T(8,128)(2,1)S(1)}, bf16[2,128,896]{2,1,0:T(8,128)(2,1)S(1)}, u32[]{:S(2)}, u32[]{:S(2)}) collective-permute-start(bf16[2,128,896]{2,1,0:T(8,128)(2,1)S(1)} %pad_maximum_fusion.1), channel_id=1, source_target_pairs={{0,2},{1,3},{2,0},{3,1},{4,6},{5,7},{6,4},{7,5},{8,10},{9,11},{10,... | collective-permute-start | bytes 1376264 | tf_op jit(solution)/shard_map/ppermute | solution.py:38
  24.7 0.8 slice_bitcast_fusion.1
  25.5 18.7 %collective-permute-done.1 = bf16[2,128,896]{2,1,0:T(8,128)(2,1)S(1)} collective-permute-done((bf16[2,128,896]{2,1,0:T(8,128)(2,1)S(1)}, bf16[2,128,896]{2,1,0:T(8,128)(2,1)S(1)}, u32[]{:S(2)}, u32[]{:S(2)}) %collective-permute-start.1) | collective-permute-done | bytes 458784 | tf_op jit(solution)/shard_map/ppermute | solution.py:38
  44.2 0.8 copy-done.13
  45.0 0.0 collective-permute-done.refs_3_
  45.0 0.0 all-to-all-done.refs_0_
  45.0 2.1 collective-permute-start.2
  47.1 2.3 %collective-permute-start.4 = (bf16[3584,128]{1,0:T(8,128)(2,1)S(1)}, bf16[3584,128]{1,0:T(8,128)(2,1)S(1)}, u32[]{:S(2)}, u32[]{:S(2)}) collective-permute-start(bf16[3584,128]{1,0:T(8,128)(2,1)S(1)} %bitcast.29), channel_id=1, source_target_pairs={{0,1},{1,0},{2,3},{3,2},{4,5},{5,4},{6,7},{7,6},{8,9},{9,8},{10,11... | collective-permute-start | bytes 2752520 | tf_op jit(solution)/shard_map/ppermute | solution.py:38
  49.4 5.0 %collective-permute-start.6 = (bf16[8,120,512]{2,1,0:T(8,128)(2,1)S(1)}, bf16[8,120,512]{2,1,0:T(8,128)(2,1)S(1)}, u32[]{:S(2)}, u32[]{:S(2)}) collective-permute-start(bf16[8,120,512]{2,1,0:T(8,128)(2,1)S(1)} %all-to-all-done.refs_0_), channel_id=1, source_target_pairs={{0,2},{1,3},{2,0},{3,1},{4,6},{5,7},{6,4},{7,5},{8,10},{9,11},{10,... | collective-permute-start | bytes 2949128 | tf_op jit(solution)/shard_map/ppermute | solution.py:38
  54.4 1.1 fusion.1
  55.5 0.0 copy-start.14
  55.5 0.1 pad_maximum_fusion.2
  55.6 2.3 %collective-permute-start.3 = (bf16[2,128,896]{2,1,0:T(8,128)(2,1)S(1)}, bf16[2,128,896]{2,1,0:T(8,128)(2,1)S(1)}, u32[]{:S(2)}, u32[]{:S(2)}) collective-permute-start(bf16[2,128,896]{2,1,0:T(8,128)(2,1)S(1)} %pad_maximum_fusion.2), channel_id=1, source_target_pairs={{0,4},{1,5},{2,6},{3,7},{4,0},{5,1},{6,2},{7,3},{8,12},{9,13},{10,... | collective-permute-start | bytes 1376264 | tf_op jit(solution)/shard_map/ppermute | solution.py:38
  58.0 1.9 collective-permute-start.5
  59.9 35.8 %collective-permute-done.5.refs_4_ = bf16[1536,128]{1,0:T(8,128)(2,1)S(1)} collective-permute-done((bf16[1536,128]{1,0:T(8,128)(2,1)S(1)}, bf16[1536,128]{1,0:T(8,128)(2,1)S(1)}, u32[]{:S(2)}, u32[]{:S(2)}) %collective-permute-start.5) | collective-permute-done | bytes 393248 | tf_op jit(solution)/shard_map/ppermute | solution.py:38
  95.7 0.0 collective-permute-done.3
  95.7 0.0 collective-permute-done.4.refs_6_
  95.7 0.0 collective-permute-done.2.refs_1_
  95.8 0.0 copy-start.2
  95.8 0.1 pad_maximum_fusion.refs_8_
  95.9 0.0 collective-permute-done.6.refs_0_
  95.9 6.0 %collective-permute-start.7 = (bf16[8,120,512]{2,1,0:T(8,128)(2,1)S(1)}, bf16[8,120,512]{2,1,0:T(8,128)(2,1)S(1)}, u32[]{:S(2)}, u32[]{:S(2)}) collective-permute-start(bf16[8,120,512]{2,1,0:T(8,128)(2,1)S(1)} %collective-permute-done.6.refs_0_), channel_id=1, source_target_pairs={{0,4},{1,5},{2,6},{3,7},{4,0},{5,1},{6,2},{7,3},{8,12},{9,13},{10,... | collective-permute-start | bytes 2949128 | tf_op jit(solution)/shard_map/ppermute | solution.py:38
  101.9 2.2 %collective-permute-start.14 = (bf16[4,128,896]{2,1,0:T(8,128)(2,1)S(1)}, bf16[4,128,896]{2,1,0:T(8,128)(2,1)}, u32[]{:S(2)}, u32[]{:S(2)}) collective-permute-start(bf16[4,128,896]{2,1,0:T(8,128)(2,1)S(1)} %pad_maximum_fusion.refs_8_), channel_id=1, source_target_pairs={{0,1},{1,0},{2,3},{3,2},{4,5},{5,4},{6,7},{7,6},{8,9},{9,8},{10,11... | collective-permute-start | bytes 2752520 | tf_op jit(solution)/shard_map/ppermute | solution.py:38
  104.2 1.2 shard_map.114.refs_0_
  105.4 1.9 collective-permute-start.8
  107.3 4.8 %collective-permute-start.9 = (bf16[272,256]{1,0:T(8,128)(2,1)S(1)}, bf16[272,256]{1,0:T(8,128)(2,1)S(1)}, u32[]{:S(2)}, u32[]{:S(2)}) collective-permute-start(bf16[272,256]{1,0:T(8,128)(2,1)S(1)} %shard_map.114.refs_0_), channel_id=1, source_target_pairs={{0,2},{1,3},{2,0},{3,1},{4,6},{5,7},{6,4},{7,5},{8,10},{9,11},{10,... | collective-permute-start | bytes 417800 | tf_op jit(solution)/shard_map/ppermute | solution.py:38
  112.1 2.6 %collective-permute-start.10 = (bf16[272,256]{1,0:T(8,128)(2,1)S(1)}, bf16[272,256]{1,0:T(8,128)(2,1)S(1)}, u32[]{:S(2)}, u32[]{:S(2)}) collective-permute-start(bf16[272,256]{1,0:T(8,128)(2,1)S(1)} %shard_map.114.refs_0_), channel_id=1, source_target_pairs={{0,6},{1,7},{2,4},{3,5},{4,2},{5,3},{6,0},{7,1},{8,14},{9,15},{10,... | collective-permute-start | bytes 417800 | tf_op jit(solution)/shard_map/ppermute | solution.py:38
  114.7 9.1 %collective-permute-done.8.refs_2_ = bf16[272,256]{1,0:T(8,128)(2,1)S(1)} collective-permute-done((bf16[272,256]{1,0:T(8,128)(2,1)S(1)}, bf16[272,256]{1,0:T(8,128)(2,1)S(1)}, u32[]{:S(2)}, u32[]{:S(2)}) %collective-permute-start.8) | collective-permute-done | bytes 139296 | tf_op jit(solution)/shard_map/ppermute | solution.py:38
  123.8 0.6 collective-permute-done.9.refs_4_
  124.4 4.0 %collective-permute-done.10.refs_6_ = bf16[272,256]{1,0:T(8,128)(2,1)S(1)} collective-permute-done((bf16[272,256]{1,0:T(8,128)(2,1)S(1)}, bf16[272,256]{1,0:T(8,128)(2,1)S(1)}, u32[]{:S(2)}, u32[]{:S(2)}) %collective-permute-start.10) | collective-permute-done | bytes 139296 | tf_op jit(solution)/shard_map/ppermute | solution.py:38
  128.4 1.2 shard_map.115.refs_1_
  129.6 2.6 %collective-permute-start.11 = (bf16[272,256]{1,0:T(8,128)(2,1)S(1)}, bf16[272,256]{1,0:T(8,128)(2,1)S(1)}, u32[]{:S(2)}, u32[]{:S(2)}) collective-permute-start(bf16[272,256]{1,0:T(8,128)(2,1)S(1)} %shard_map.115.refs_1_), channel_id=1, source_target_pairs={{0,4},{1,5},{2,6},{3,7},{4,0},{5,1},{6,2},{7,3},{8,12},{9,13},{10,... | collective-permute-start | bytes 417800 | tf_op jit(solution)/shard_map/ppermute | solution.py:38
  132.3 2.6 %collective-permute-start.12 = (bf16[272,256]{1,0:T(8,128)(2,1)S(1)}, bf16[272,256]{1,0:T(8,128)(2,1)S(1)}, u32[]{:S(2)}, u32[]{:S(2)}) collective-permute-start(bf16[272,256]{1,0:T(8,128)(2,1)S(1)} %shard_map.115.refs_1_), channel_id=1, source_target_pairs={{0,2},{1,3},{2,0},{3,1},{4,6},{5,7},{6,4},{7,5},{8,10},{9,11},{10,... | collective-permute-start | bytes 417800 | tf_op jit(solution)/shard_map/ppermute | solution.py:38
  134.9 4.0 %collective-permute-start.13 = (bf16[272,256]{1,0:T(8,128)(2,1)S(1)}, bf16[272,256]{1,0:T(8,128)(2,1)S(1)}, u32[]{:S(2)}, u32[]{:S(2)}) collective-permute-start(bf16[272,256]{1,0:T(8,128)(2,1)S(1)} %shard_map.115.refs_1_), channel_id=1, source_target_pairs={{0,6},{1,7},{2,4},{3,5},{4,2},{5,3},{6,0},{7,1},{8,14},{9,15},{10,... | collective-permute-start | bytes 417800 | tf_op jit(solution)/shard_map/ppermute | solution.py:38
  138.9 0.1 pad_add_fusion.places
  139.0 1.5 collective-permute-done.12.refs_5_
  140.5 3.7 %collective-permute-done.13.refs_7_ = bf16[272,256]{1,0:T(8,128)(2,1)S(1)} collective-permute-done((bf16[272,256]{1,0:T(8,128)(2,1)S(1)}, bf16[272,256]{1,0:T(8,128)(2,1)S(1)}, u32[]{:S(2)}, u32[]{:S(2)}) %collective-permute-start.13) | collective-permute-done | bytes 139296 | tf_op jit(solution)/shard_map/ppermute | solution.py:38
  144.2 3.6 %shard_map.116 = bf16[16,2,120,128]{3,2,1,0:T(8,128)(2,1)} custom-call(s32[4]{0:T(128)S(1)} %pad_add_fusion.places, bf16[272,256]{1,0:T(8,128)(2,1)S(1)} %shard_map.114.refs_0_, bf16[272,256]{1,0:T(8,128)(2,1)S(1)} %shard_map.115.refs_1_, bf16[272,256]{1,0:T(8,128)(2,1)S(1)} %collective-permute-done.8.refs_2_, ...), custom_call_target="tpu_custom_call" | custom-call | tf_op jit(solution)/shard_map/pallas_call | solution.py:169
  147.8 7.0 %all-to-all-start.1 = ((bf16[16,2,120,128]{3,2,1,0:T(8,128)(2,1)}), bf16[16,2,120,128]{3,2,1,0:T(8,128)(2,1)S(1)}, u32[]{:S(2)}, u32[]{:S(2)}) async-start(bf16[16,2,120,128]{3,2,1,0:T(8,128)(2,1)} %shard_map.116), calls=%async_computation.1 | async-start | bytes 1966080 | tf_op jit(solution)/shard_map/all_to_all | solution.py:275
  154.8 0.0 copy-start.15
  154.8 0.6 copy-done.15
  155.4 0.1 copy.12.gate_ref
  155.5 0.7 copy-done.16
  156.2 0.1 copy.13.gate_ref
  156.3 17.6 %all-to-all-done.1.got_ref = bf16[16,2,120,128]{3,2,1,0:T(8,128)(2,1)S(1)} async-done(((bf16[16,2,120,128]{3,2,1,0:T(8,128)(2,1)}), bf16[16,2,120,128]{3,2,1,0:T(8,128)(2,1)S(1)}, u32[]{:S(2)}, u32[]{:S(2)}) %all-to-all-start.1) | async-done | bytes 983072 | tf_op jit(solution)/shard_map/all_to_all | solution.py:275
  173.9 0.6 shard_map.117
  174.5 18.3 %collective-permute-start.15 = (bf16[1,64,3584]{2,1,0:T(8,128)(2,1)S(1)}, bf16[1,64,3584]{2,1,0:T(8,128)(2,1)S(1)}, u32[]{:S(2)}, u32[]{:S(2)}) collective-permute-start(bf16[1,64,3584]{2,1,0:T(8,128)(2,1)S(1)} %bitcast.36), channel_id=1, source_target_pairs={{0,32},{32,64},{64,96},{96,128},{128,160},{160,192},{192,224},{224... | collective-permute-start | bytes 1376264 | tf_op jit(solution)/shard_map/ppermute | solution.py:33
  192.8 0.6 shard_map.118
  193.4 1.9 collective-permute-start.16
  195.4 6.5 %collective-permute-done.15 = bf16[1,64,3584]{2,1,0:T(8,128)(2,1)S(1)} collective-permute-done((bf16[1,64,3584]{2,1,0:T(8,128)(2,1)S(1)}, bf16[1,64,3584]{2,1,0:T(8,128)(2,1)S(1)}, u32[]{:S(2)}, u32[]{:S(2)}) %collective-permute-start.15) | collective-permute-done | bytes 458784 | tf_op jit(solution)/shard_map/ppermute | solution.py:33
  201.9 11.2 %collective-permute-done.16 = bf16[1,64,3584]{2,1,0:T(8,128)(2,1)S(1)} collective-permute-done((bf16[1,64,3584]{2,1,0:T(8,128)(2,1)S(1)}, bf16[1,64,3584]{2,1,0:T(8,128)(2,1)S(1)}, u32[]{:S(2)}, u32[]{:S(2)}) %collective-permute-start.16) | collective-permute-done | bytes 458784 | tf_op jit(solution)/shard_map/ppermute | solution.py:33
  213.0 0.8 copy.16
  213.8 0.8 copy.17
  (27 shorter events, 0.1 us)
Async XLA Ops:
  0.6 0.7 copy-start.8
  0.6 0.7 copy-start.9
  1.3 1.0 copy-start.3
  2.3 1.0 copy-start.5
  3.3 0.7 copy-start.7
  5.9 7.0 %copy-start = (bf16[1,3584,128]{2,1,0:T(8,128)(2,1)S(1)}, bf16[1,3584,128]{2,1,0:T(8,128)(2,1)}, u32[]{:S(2)}) copy-start(bf16[1,3584,128]{2,1,0:T(8,128)(2,1)} %param.17) | copy-start | bytes 2752516
  5.9 39.1 %all-to-all-start = ((bf16[8,120,512]{2,1,0:T(8,128)(2,1)}), bf16[8,120,512]{2,1,0:T(8,128)(2,1)S(1)}, u32[]{:S(2)}, u32[]{:S(2)}) async-start(bf16[8,120,512]{2,1,0:T(8,128)(2,1)} %shard_map.113), calls=%async_computation | async-start | bytes 1966080 | tf_op jit(solution)/shard_map/all_to_all | solution.py:238
  12.9 4.9 %copy-start.10 = (bf16[1,128,3584]{2,1,0:T(8,128)(2,1)S(1)}, bf16[1,128,3584]{2,1,0:T(8,128)(2,1)}, u32[]{:S(2)}) copy-start(bf16[1,128,3584]{2,1,0:T(8,128)(2,1)} %param.19) | copy-start | bytes 2752516
  13.7 31.3 %collective-permute-start = (bf16[2048,128]{1,0:T(8,128)(2,1)}, bf16[2048,128]{1,0:T(8,128)(2,1)S(1)}, u32[]{:S(2)}, u32[]{:S(2)}) collective-permute-start(bf16[2048,128]{1,0:T(8,128)(2,1)} %slice_bitcast_fusion), channel_id=1, source_target_pairs={{0,1},{1,0},{2,3},{3,2},{4,5},{5,4},{6,7},{7,6},{8,9},{9,8},{10,11... | collective-permute-start | bytes 1572872 | tf_op jit(solution)/shard_map/ppermute | solution.py:38
  18.7 28.3 %copy-start.1 = (bf16[1,3584,128]{2,1,0:T(8,128)(2,1)S(1)}, bf16[1,3584,128]{2,1,0:T(8,128)(2,1)}, u32[]{:S(2)}) copy-start(bf16[1,3584,128]{2,1,0:T(8,128)(2,1)} %param.18) | copy-start | bytes 2752516
  18.8 25.5 %collective-permute-start.1 = (bf16[2,128,896]{2,1,0:T(8,128)(2,1)S(1)}, bf16[2,128,896]{2,1,0:T(8,128)(2,1)S(1)}, u32[]{:S(2)}, u32[]{:S(2)}) collective-permute-start(bf16[2,128,896]{2,1,0:T(8,128)(2,1)S(1)} %pad_maximum_fusion.1), channel_id=1, source_target_pairs={{0,2},{1,3},{2,0},{3,1},{4,6},{5,7},{6,4},{7,5},{8,10},{9,11},{10,... | collective-permute-start | bytes 1376264 | tf_op jit(solution)/shard_map/ppermute | solution.py:38
  44.2 0.8 copy-start.13
  45.0 10.5 %copy-start.12 = (bf16[1,128,896]{2,1,0:T(8,128)(2,1)S(1)}, bf16[1,128,896]{2,1,0:T(8,128)(2,1)}, u32[]{:S(2)}) copy-start(bf16[1,128,896]{2,1,0:T(8,128)(2,1)} %get-tuple-element.34) | copy-start | bytes 688132
  45.0 50.7 %collective-permute-start.2 = (bf16[8,120,512]{2,1,0:T(8,128)(2,1)S(1)}, bf16[8,120,512]{2,1,0:T(8,128)(2,1)S(1)}, u32[]{:S(2)}, u32[]{:S(2)}) collective-permute-start(bf16[8,120,512]{2,1,0:T(8,128)(2,1)S(1)} %all-to-all-done.refs_0_), channel_id=1, source_target_pairs={{0,4},{1,5},{2,6},{3,7},{4,0},{5,1},{6,2},{7,3},{8,12},{9,13},{10,... | collective-permute-start | bytes 2949128 | tf_op jit(solution)/shard_map/ppermute | solution.py:38
  47.1 48.6 %collective-permute-start.4 = (bf16[3584,128]{1,0:T(8,128)(2,1)S(1)}, bf16[3584,128]{1,0:T(8,128)(2,1)S(1)}, u32[]{:S(2)}, u32[]{:S(2)}) collective-permute-start(bf16[3584,128]{1,0:T(8,128)(2,1)S(1)} %bitcast.29), channel_id=1, source_target_pairs={{0,1},{1,0},{2,3},{3,2},{4,5},{5,4},{6,7},{7,6},{8,9},{9,8},{10,11... | collective-permute-start | bytes 2752520 | tf_op jit(solution)/shard_map/ppermute | solution.py:38
  49.4 46.5 %collective-permute-start.6 = (bf16[8,120,512]{2,1,0:T(8,128)(2,1)S(1)}, bf16[8,120,512]{2,1,0:T(8,128)(2,1)S(1)}, u32[]{:S(2)}, u32[]{:S(2)}) collective-permute-start(bf16[8,120,512]{2,1,0:T(8,128)(2,1)S(1)} %all-to-all-done.refs_0_), channel_id=1, source_target_pairs={{0,2},{1,3},{2,0},{3,1},{4,6},{5,7},{6,4},{7,5},{8,10},{9,11},{10,... | collective-permute-start | bytes 2949128 | tf_op jit(solution)/shard_map/ppermute | solution.py:38
  55.5 2.4 %copy-start.14 = (bf16[1536,128]{1,0:T(8,128)(2,1)S(1)}, bf16[1536,128]{1,0:T(8,128)(2,1)}, u32[]{:S(2)}) copy-start(bf16[1536,128]{1,0:T(8,128)(2,1)} %slice_bitcast_fusion.1) | copy-start | bytes 1179652
  55.6 40.2 %copy-start.11 = (bf16[1,128,896]{2,1,0:T(8,128)(2,1)S(1)}, bf16[1,128,896]{2,1,0:T(8,128)(2,1)}, u32[]{:S(2)}) copy-start(bf16[1,128,896]{2,1,0:T(8,128)(2,1)} %get-tuple-element.32) | copy-start | bytes 688132
  55.6 40.1 %collective-permute-start.3 = (bf16[2,128,896]{2,1,0:T(8,128)(2,1)S(1)}, bf16[2,128,896]{2,1,0:T(8,128)(2,1)S(1)}, u32[]{:S(2)}, u32[]{:S(2)}) collective-permute-start(bf16[2,128,896]{2,1,0:T(8,128)(2,1)S(1)} %pad_maximum_fusion.2), channel_id=1, source_target_pairs={{0,4},{1,5},{2,6},{3,7},{4,0},{5,1},{6,2},{7,3},{8,12},{9,13},{10,... | collective-permute-start | bytes 1376264 | tf_op jit(solution)/shard_map/ppermute | solution.py:38
  58.0 37.7 %collective-permute-start.5 = (bf16[1536,128]{1,0:T(8,128)(2,1)S(1)}, bf16[1536,128]{1,0:T(8,128)(2,1)S(1)}, u32[]{:S(2)}, u32[]{:S(2)}) collective-permute-start(bf16[1536,128]{1,0:T(8,128)(2,1)S(1)} %copy-done.14), channel_id=1, source_target_pairs={{0,1},{1,0},{2,3},{3,2},{4,5},{5,4},{6,7},{7,6},{8,9},{9,8},{10,11... | collective-permute-start | bytes 1179656 | tf_op jit(solution)/shard_map/ppermute | solution.py:38
  95.8 8.4 %copy-start.2 = (bf16[1,3584,128]{2,1,0:T(8,128)(2,1)S(1)}, bf16[1,3584,128]{2,1,0:T(8,128)(2,1)}, u32[]{:S(2)}) copy-start(bf16[1,3584,128]{2,1,0:T(8,128)(2,1)} %param.18) | copy-start | bytes 2752516
  95.9 32.5 %collective-permute-start.7 = (bf16[8,120,512]{2,1,0:T(8,128)(2,1)S(1)}, bf16[8,120,512]{2,1,0:T(8,128)(2,1)S(1)}, u32[]{:S(2)}, u32[]{:S(2)}) collective-permute-start(bf16[8,120,512]{2,1,0:T(8,128)(2,1)S(1)} %collective-permute-done.6.refs_0_), channel_id=1, source_target_pairs={{0,4},{1,5},{2,6},{3,7},{4,0},{5,1},{6,2},{7,3},{8,12},{9,13},{10,... | collective-permute-start | bytes 2949128 | tf_op jit(solution)/shard_map/ppermute | solution.py:38
  101.9 37.1 %collective-permute-start.14 = (bf16[4,128,896]{2,1,0:T(8,128)(2,1)S(1)}, bf16[4,128,896]{2,1,0:T(8,128)(2,1)}, u32[]{:S(2)}, u32[]{:S(2)}) collective-permute-start(bf16[4,128,896]{2,1,0:T(8,128)(2,1)S(1)} %pad_maximum_fusion.refs_8_), channel_id=1, source_target_pairs={{0,1},{1,0},{2,3},{3,2},{4,5},{5,4},{6,7},{7,6},{8,9},{9,8},{10,11... | collective-permute-start | bytes 2752520 | tf_op jit(solution)/shard_map/ppermute | solution.py:38
  105.4 18.4 %collective-permute-start.8 = (bf16[272,256]{1,0:T(8,128)(2,1)S(1)}, bf16[272,256]{1,0:T(8,128)(2,1)S(1)}, u32[]{:S(2)}, u32[]{:S(2)}) collective-permute-start(bf16[272,256]{1,0:T(8,128)(2,1)S(1)} %shard_map.114.refs_0_), channel_id=1, source_target_pairs={{0,4},{1,5},{2,6},{3,7},{4,0},{5,1},{6,2},{7,3},{8,12},{9,13},{10,... | collective-permute-start | bytes 417800 | tf_op jit(solution)/shard_map/ppermute | solution.py:38
  107.3 17.1 %collective-permute-start.9 = (bf16[272,256]{1,0:T(8,128)(2,1)S(1)}, bf16[272,256]{1,0:T(8,128)(2,1)S(1)}, u32[]{:S(2)}, u32[]{:S(2)}) collective-permute-start(bf16[272,256]{1,0:T(8,128)(2,1)S(1)} %shard_map.114.refs_0_), channel_id=1, source_target_pairs={{0,2},{1,3},{2,0},{3,1},{4,6},{5,7},{6,4},{7,5},{8,10},{9,11},{10,... | collective-permute-start | bytes 417800 | tf_op jit(solution)/shard_map/ppermute | solution.py:38
  112.1 16.3 %collective-permute-start.10 = (bf16[272,256]{1,0:T(8,128)(2,1)S(1)}, bf16[272,256]{1,0:T(8,128)(2,1)S(1)}, u32[]{:S(2)}, u32[]{:S(2)}) collective-permute-start(bf16[272,256]{1,0:T(8,128)(2,1)S(1)} %shard_map.114.refs_0_), channel_id=1, source_target_pairs={{0,6},{1,7},{2,4},{3,5},{4,2},{5,3},{6,0},{7,1},{8,14},{9,15},{10,... | collective-permute-start | bytes 417800 | tf_op jit(solution)/shard_map/ppermute | solution.py:38
  129.6 9.4 %collective-permute-start.11 = (bf16[272,256]{1,0:T(8,128)(2,1)S(1)}, bf16[272,256]{1,0:T(8,128)(2,1)S(1)}, u32[]{:S(2)}, u32[]{:S(2)}) collective-permute-start(bf16[272,256]{1,0:T(8,128)(2,1)S(1)} %shard_map.115.refs_1_), channel_id=1, source_target_pairs={{0,4},{1,5},{2,6},{3,7},{4,0},{5,1},{6,2},{7,3},{8,12},{9,13},{10,... | collective-permute-start | bytes 417800 | tf_op jit(solution)/shard_map/ppermute | solution.py:38
  132.3 8.2 %collective-permute-start.12 = (bf16[272,256]{1,0:T(8,128)(2,1)S(1)}, bf16[272,256]{1,0:T(8,128)(2,1)S(1)}, u32[]{:S(2)}, u32[]{:S(2)}) collective-permute-start(bf16[272,256]{1,0:T(8,128)(2,1)S(1)} %shard_map.115.refs_1_), channel_id=1, source_target_pairs={{0,2},{1,3},{2,0},{3,1},{4,6},{5,7},{6,4},{7,5},{8,10},{9,11},{10,... | collective-permute-start | bytes 417800 | tf_op jit(solution)/shard_map/ppermute | solution.py:38
  134.9 9.3 %collective-permute-start.13 = (bf16[272,256]{1,0:T(8,128)(2,1)S(1)}, bf16[272,256]{1,0:T(8,128)(2,1)S(1)}, u32[]{:S(2)}, u32[]{:S(2)}) collective-permute-start(bf16[272,256]{1,0:T(8,128)(2,1)S(1)} %shard_map.115.refs_1_), channel_id=1, source_target_pairs={{0,6},{1,7},{2,4},{3,5},{4,2},{5,3},{6,0},{7,1},{8,14},{9,15},{10,... | collective-permute-start | bytes 417800 | tf_op jit(solution)/shard_map/ppermute | solution.py:38
  147.8 26.1 %copy-start.4 = (bf16[1,64,3584]{2,1,0:T(8,128)(2,1)S(1)}, bf16[1,64,3584]{2,1,0:T(8,128)(2,1)}, u32[]{:S(2)}) copy-start(bf16[1,64,3584]{2,1,0:T(8,128)(2,1)} %param.10) | copy-start | bytes 1376260
  147.8 26.1 %all-to-all-start.1 = ((bf16[16,2,120,128]{3,2,1,0:T(8,128)(2,1)}), bf16[16,2,120,128]{3,2,1,0:T(8,128)(2,1)S(1)}, u32[]{:S(2)}, u32[]{:S(2)}) async-start(bf16[16,2,120,128]{3,2,1,0:T(8,128)(2,1)} %shard_map.116), calls=%async_computation.1 | async-start | bytes 1966080 | tf_op jit(solution)/shard_map/all_to_all | solution.py:275
  154.8 0.7 copy-start.15
  155.5 0.7 copy-start.16
  156.3 36.5 %copy-start.6 = (bf16[1,64,3584]{2,1,0:T(8,128)(2,1)S(1)}, bf16[1,64,3584]{2,1,0:T(8,128)(2,1)}, u32[]{:S(2)}) copy-start(bf16[1,64,3584]{2,1,0:T(8,128)(2,1)} %param.11) | copy-start | bytes 1376260
  174.5 27.4 %collective-permute-start.15 = (bf16[1,64,3584]{2,1,0:T(8,128)(2,1)S(1)}, bf16[1,64,3584]{2,1,0:T(8,128)(2,1)S(1)}, u32[]{:S(2)}, u32[]{:S(2)}) collective-permute-start(bf16[1,64,3584]{2,1,0:T(8,128)(2,1)S(1)} %bitcast.36), channel_id=1, source_target_pairs={{0,32},{32,64},{64,96},{96,128},{128,160},{160,192},{192,224},{224... | collective-permute-start | bytes 1376264 | tf_op jit(solution)/shard_map/ppermute | solution.py:33
  193.4 19.6 %collective-permute-start.16 = (bf16[1,64,3584]{2,1,0:T(8,128)(2,1)S(1)}, bf16[1,64,3584]{2,1,0:T(8,128)(2,1)S(1)}, u32[]{:S(2)}, u32[]{:S(2)}) collective-permute-start(bf16[1,64,3584]{2,1,0:T(8,128)(2,1)S(1)} %bitcast.37), channel_id=1, source_target_pairs={{0,480},{32,0},{64,32},{96,64},{128,96},{160,128},{192,160},{224,1... | collective-permute-start | bytes 1376264 | tf_op jit(solution)/shard_map/ppermute | solution.py:33

commit v4 on v3

--- a/solution.py
+++ b/solution.py
@@ -248,9 +248,9 @@
     weights = (gate_w, gate_low, gate_high, up_w, up_b)
     early = hidden_of((own, beside), weights)
     down_a = jnp.stack([parts[0], from_twin[0], from_far[0], from_twin[1]])
-    far_rows, down_a = step((far_rows, down_a))
+    early_sent = [swapped(early, TEAM[k]) for k in range(1, RUN)]
+    early_sent[0], down_a = step((early_sent[0], down_a))
     down_b = swapped(down_a, NEAR)
-    early_sent = [swapped(early, TEAM[k]) for k in range(1, RUN)]
     far_last = swapped(far_rows, TEAM[1])
     far_last, early_sent = step((far_last, early_sent))
     late = hidden_of((far_rows, far_last), weights)

time: 216 us -> 223 us (1.032)
  waiting for transfers between devices: 109 us -> 116 us
  starting transfers between devices: 84.5 us -> 79.5 us
  local copies, waits for them, and re-layouts: 9.96 us -> 12.7 us
    ppermute x15, waiting for transfers between devices: 73.5 us -> 80 us  [swapped(): return lax.ppermute(shard, 'expert', [(i, i ^ bits) for i in range(size)])]
    all_to_all x1, starting transfers between devices: 6.98 us -> 3.95 us  [on_device(): lax.all_to_all(back, 'expert', 0, 0, axis_index_groups=halves, tiled=True)]
    unnamed x36 -> x46, local copies, waits for them, and re-layouts: 7.05 us -> 9.78 us
  transfers between devices with their start and end apart: 19 -> 19, of which waited for: 10 -> 9; matrix products, arithmetic and copies ran while one was open for 2% -> 2% of each run, Pallas kernels for 1% -> 2%
where the time goes in v4:
time: 223 us; the launch traced here: 220 us
  waiting for transfers between devices  116 us (52%)
  starting transfers between devices  79.5 us (36%)
  local copies, waits for them, and re-layouts  12.7 us (6%)
  Pallas kernels  9.79 us (4%)
    ppermute x15, waiting for transfers between devices, swapped(): return lax.ppermute(shard, 'expert', [(i, i ^ bits) for i in range(size)])  80 us
    ppermute x15, starting transfers between devices, swapped(): return lax.ppermute(shard, 'expert', [(i, i ^ bits) for i in range(size)])  49.3 us
    ppermute x2, starting transfers between devices, shifted(): lax.ppermute(shard, axis, [(i, (i + by) % size) for i in range(size)])  19.4 us
    all_to_all x1, waiting for transfers between devices, on_device(): lax.all_to_all(back, 'expert', 0, 0, axis_index_groups=halves, tiled=True)  18.2 us
    ppermute x2, waiting for transfers between devices, shifted(): lax.ppermute(shard, axis, [(i, (i + by) % size) for i in range(size)])  17.3 us
    pallas_call x6, Pallas kernels, call(): pl.pallas_call(kernel, out_shape=jax.ShapeDtypeStruct(shape, dtype), in_s...  9.79 us
    unnamed x46, local copies, waits for them, and re-layouts  9.78 us
    all_to_all x1, starting transfers between devices, on_device(): lax.all_to_all(sent, 'expert', 0, 0, axis_index_groups=columns, tiled=True)  6.95 us
  transfers between devices with their start and end apart: 19, of which 9 were waited for; matrix products, arithmetic and copies ran while one was open for 2% of the time, Pallas kernels for 2%

profile of v4, /device:TPU:7, one launch (start us, length us, event | category | flops | bytes accessed | tf_op | source)
XLA Modules:
  0.0 219.8 jit_solution(14968784314234480700)
XLA Ops:
  0.7 0.6 copy-done.13
  1.3 0.0 copy-done.14
  1.3 1.0 copy-done.2
  2.3 1.0 copy-done.4
  3.3 0.7 copy-done.12
  4.1 1.9 shard_map.113
  5.9 7.0 %all-to-all-start = ((bf16[8,120,512]{2,1,0:T(8,128)(2,1)}), bf16[8,120,512]{2,1,0:T(8,128)(2,1)S(1)}, u32[]{:S(2)}, u32[]{:S(2)}) async-start(bf16[8,120,512]{2,1,0:T(8,128)(2,1)} %shard_map.113), calls=%async_computation | async-start | bytes 1966080 | tf_op jit(solution)/shard_map/all_to_all | solution.py:238
  12.9 0.0 copy-start.15
  12.9 0.8 slice_bitcast_fusion
  13.7 4.0 %collective-permute-start = (bf16[2048,128]{1,0:T(8,128)(2,1)}, bf16[2048,128]{1,0:T(8,128)(2,1)S(1)}, u32[]{:S(2)}, u32[]{:S(2)}) collective-permute-start(bf16[2048,128]{1,0:T(8,128)(2,1)} %slice_bitcast_fusion), channel_id=1, source_target_pairs={{0,1},{1,0},{2,3},{3,2},{4,5},{5,4},{6,7},{7,6},{8,9},{9,8},{10,11... | collective-permute-start | bytes 1572872 | tf_op jit(solution)/shard_map/ppermute | solution.py:38
  17.8 0.9 select_bitcast_fusion
  18.8 5.9 %collective-permute-start.1 = (bf16[2,128,896]{2,1,0:T(8,128)(2,1)S(1)}, bf16[2,128,896]{2,1,0:T(8,128)(2,1)S(1)}, u32[]{:S(2)}, u32[]{:S(2)}) collective-permute-start(bf16[2,128,896]{2,1,0:T(8,128)(2,1)S(1)} %pad_maximum_fusion.1), channel_id=1, source_target_pairs={{0,2},{1,3},{2,0},{3,1},{4,6},{5,7},{6,4},{7,5},{8,10},{9,11},{10,... | collective-permute-start | bytes 1376264 | tf_op jit(solution)/shard_map/ppermute | solution.py:38
  24.7 0.8 slice_bitcast_fusion.1
  25.5 18.7 %collective-permute-done.1 = bf16[2,128,896]{2,1,0:T(8,128)(2,1)S(1)} collective-permute-done((bf16[2,128,896]{2,1,0:T(8,128)(2,1)S(1)}, bf16[2,128,896]{2,1,0:T(8,128)(2,1)S(1)}, u32[]{:S(2)}, u32[]{:S(2)}) %collective-permute-start.1) | collective-permute-done | bytes 458784 | tf_op jit(solution)/shard_map/ppermute | solution.py:38
  44.2 0.8 copy-done.18
  45.0 0.0 collective-permute-done.refs_3_
  45.0 0.0 all-to-all-done.refs_0_
  45.0 2.1 collective-permute-start.2
  47.1 1.9 collective-permute-start.6
  49.0 5.4 %collective-permute-start.4 = (bf16[3584,128]{1,0:T(8,128)(2,1)S(1)}, bf16[3584,128]{1,0:T(8,128)(2,1)S(1)}, u32[]{:S(2)}, u32[]{:S(2)}) collective-permute-start(bf16[3584,128]{1,0:T(8,128)(2,1)S(1)} %bitcast.29), channel_id=1, source_target_pairs={{0,1},{1,0},{2,3},{3,2},{4,5},{5,4},{6,7},{7,6},{8,9},{9,8},{10,11... | collective-permute-start | bytes 2752520 | tf_op jit(solution)/shard_map/ppermute | solution.py:38
  54.4 1.1 fusion.1
  55.5 0.0 copy-start.19
  55.5 0.1 pad_maximum_fusion.2
  55.6 2.4 %collective-permute-start.3 = (bf16[2,128,896]{2,1,0:T(8,128)(2,1)S(1)}, bf16[2,128,896]{2,1,0:T(8,128)(2,1)S(1)}, u32[]{:S(2)}, u32[]{:S(2)}) collective-permute-start(bf16[2,128,896]{2,1,0:T(8,128)(2,1)S(1)} %pad_maximum_fusion.2), channel_id=1, source_target_pairs={{0,4},{1,5},{2,6},{3,7},{4,0},{5,1},{6,2},{7,3},{8,12},{9,13},{10,... | collective-permute-start | bytes 1376264 | tf_op jit(solution)/shard_map/ppermute | solution.py:38
  58.0 1.9 collective-permute-start.5
  59.9 41.0 %collective-permute-done.5.refs_4_ = bf16[1536,128]{1,0:T(8,128)(2,1)S(1)} collective-permute-done((bf16[1536,128]{1,0:T(8,128)(2,1)S(1)}, bf16[1536,128]{1,0:T(8,128)(2,1)S(1)}, u32[]{:S(2)}, u32[]{:S(2)}) %collective-permute-start.5) | collective-permute-done | bytes 393248 | tf_op jit(solution)/shard_map/ppermute | solution.py:38
  100.9 0.0 collective-permute-done.3
  100.9 0.0 collective-permute-done.4.refs_6_
  100.9 0.0 collective-permute-done.2.refs_1_
  100.9 1.2 shard_map.114.refs_0_
  102.1 3.5 %collective-permute-start.8 = (bf16[272,256]{1,0:T(8,128)(2,1)S(1)}, bf16[272,256]{1,0:T(8,128)(2,1)S(1)}, u32[]{:S(2)}, u32[]{:S(2)}) collective-permute-start(bf16[272,256]{1,0:T(8,128)(2,1)S(1)} %shard_map.114.refs_0_), channel_id=1, source_target_pairs={{0,4},{1,5},{2,6},{3,7},{4,0},{5,1},{6,2},{7,3},{8,12},{9,13},{10,... | collective-permute-start | bytes 417800 | tf_op jit(solution)/shard_map/ppermute | solution.py:38
  105.7 1.9 collective-permute-start.7
  107.7 0.1 pad_maximum_fusion.refs_8_
  107.8 0.3 collective-permute-done.8.refs_2_
  108.1 1.9 collective-permute-start.14
  110.0 4.2 %collective-permute-start.9 = (bf16[272,256]{1,0:T(8,128)(2,1)S(1)}, bf16[272,256]{1,0:T(8,128)(2,1)S(1)}, u32[]{:S(2)}, u32[]{:S(2)}) collective-permute-start(bf16[272,256]{1,0:T(8,128)(2,1)S(1)} %shard_map.114.refs_0_), channel_id=1, source_target_pairs={{0,2},{1,3},{2,0},{3,1},{4,6},{5,7},{6,4},{7,5},{8,10},{9,11},{10,... | collective-permute-start | bytes 417800 | tf_op jit(solution)/shard_map/ppermute | solution.py:38
  114.2 3.1 %collective-permute-start.10 = (bf16[272,256]{1,0:T(8,128)(2,1)S(1)}, bf16[272,256]{1,0:T(8,128)(2,1)S(1)}, u32[]{:S(2)}, u32[]{:S(2)}) collective-permute-start(bf16[272,256]{1,0:T(8,128)(2,1)S(1)} %shard_map.114.refs_0_), channel_id=1, source_target_pairs={{0,6},{1,7},{2,4},{3,5},{4,2},{5,3},{6,0},{7,1},{8,14},{9,15},{10,... | collective-permute-start | bytes 417800 | tf_op jit(solution)/shard_map/ppermute | solution.py:38
  117.4 9.7 %collective-permute-done.9.refs_4_ = bf16[272,256]{1,0:T(8,128)(2,1)S(1)} collective-permute-done((bf16[272,256]{1,0:T(8,128)(2,1)S(1)}, bf16[272,256]{1,0:T(8,128)(2,1)S(1)}, u32[]{:S(2)}, u32[]{:S(2)}) %collective-permute-start.9) | collective-permute-done | bytes 139296 | tf_op jit(solution)/shard_map/ppermute | solution.py:38
  127.1 4.7 %collective-permute-done.10.refs_6_ = bf16[272,256]{1,0:T(8,128)(2,1)S(1)} collective-permute-done((bf16[272,256]{1,0:T(8,128)(2,1)S(1)}, bf16[272,256]{1,0:T(8,128)(2,1)S(1)}, u32[]{:S(2)}, u32[]{:S(2)}) %collective-permute-start.10) | collective-permute-done | bytes 139296 | tf_op jit(solution)/shard_map/ppermute | solution.py:38
  131.7 1.8 shard_map.115.refs_1_
  133.6 2.9 %collective-permute-start.11 = (bf16[272,256]{1,0:T(8,128)(2,1)}, bf16[272,256]{1,0:T(8,128)(2,1)S(1)}, u32[]{:S(2)}, u32[]{:S(2)}) collective-permute-start(bf16[272,256]{1,0:T(8,128)(2,1)} %shard_map.115.refs_1_), channel_id=1, source_target_pairs={{0,4},{1,5},{2,6},{3,7},{4,0},{5,1},{6,2},{7,3},{8,12},{9,13},{10,... | collective-permute-start | bytes 417800 | tf_op jit(solution)/shard_map/ppermute | solution.py:38
  136.5 5.0 %collective-permute-start.12 = (bf16[272,256]{1,0:T(8,128)(2,1)}, bf16[272,256]{1,0:T(8,128)(2,1)S(1)}, u32[]{:S(2)}, u32[]{:S(2)}) collective-permute-start(bf16[272,256]{1,0:T(8,128)(2,1)} %shard_map.115.refs_1_), channel_id=1, source_target_pairs={{0,2},{1,3},{2,0},{3,1},{4,6},{5,7},{6,4},{7,5},{8,10},{9,11},{10,... | collective-permute-start | bytes 417800 | tf_op jit(solution)/shard_map/ppermute | solution.py:38
  141.5 3.1 %collective-permute-start.13 = (bf16[272,256]{1,0:T(8,128)(2,1)}, bf16[272,256]{1,0:T(8,128)(2,1)S(1)}, u32[]{:S(2)}, u32[]{:S(2)}) collective-permute-start(bf16[272,256]{1,0:T(8,128)(2,1)} %shard_map.115.refs_1_), channel_id=1, source_target_pairs={{0,6},{1,7},{2,4},{3,5},{4,2},{5,3},{6,0},{7,1},{8,14},{9,15},{10,... | collective-permute-start | bytes 417800 | tf_op jit(solution)/shard_map/ppermute | solution.py:38
  144.6 0.1 pad_add_fusion.places
  144.7 5.6 %collective-permute-done.13.refs_7_ = bf16[272,256]{1,0:T(8,128)(2,1)S(1)} collective-permute-done((bf16[272,256]{1,0:T(8,128)(2,1)}, bf16[272,256]{1,0:T(8,128)(2,1)S(1)}, u32[]{:S(2)}, u32[]{:S(2)}) %collective-permute-start.13) | collective-permute-done | bytes 139296 | tf_op jit(solution)/shard_map/ppermute | solution.py:38
  150.3 0.9 copy-done.7
  151.2 0.9 copy-done.9
  152.1 0.9 copy-done.11
  153.0 3.7 %shard_map.116 = bf16[16,2,120,128]{3,2,1,0:T(8,128)(2,1)} custom-call(s32[4]{0:T(128)S(1)} %pad_add_fusion.places, bf16[272,256]{1,0:T(8,128)(2,1)S(1)} %shard_map.114.refs_0_, bf16[272,256]{1,0:T(8,128)(2,1)} %shard_map.115.refs_1_, bf16[272,256]{1,0:T(8,128)(2,1)S(1)} %copy-done.7, bf16[272,256]{1,0:T(8,128)(2,1)S(1)} %collective-permute-done.11.refs_3_, ...), custom_call_target="tpu_custom_call" | custom-call | tf_op jit(solution)/shard_map/pallas_call | solution.py:169
  156.7 3.9 %all-to-all-start.1 = ((bf16[16,2,120,128]{3,2,1,0:T(8,128)(2,1)}), bf16[16,2,120,128]{3,2,1,0:T(8,128)(2,1)S(1)}, u32[]{:S(2)}, u32[]{:S(2)}) async-start(bf16[16,2,120,128]{3,2,1,0:T(8,128)(2,1)} %shard_map.116), calls=%async_computation.1 | async-start | bytes 1966080 | tf_op jit(solution)/shard_map/all_to_all | solution.py:275
  160.7 0.0 copy-start.20
  160.7 0.6 copy-done.20
  161.3 0.1 copy.12.gate_ref
  161.4 0.7 copy-done.21
  162.1 0.1 copy.13.gate_ref
  162.2 18.2 %all-to-all-done.1.got_ref = bf16[16,2,120,128]{3,2,1,0:T(8,128)(2,1)S(1)} async-done(((bf16[16,2,120,128]{3,2,1,0:T(8,128)(2,1)}), bf16[16,2,120,128]{3,2,1,0:T(8,128)(2,1)S(1)}, u32[]{:S(2)}, u32[]{:S(2)}) %all-to-all-start.1) | async-done | bytes 983072 | tf_op jit(solution)/shard_map/all_to_all | solution.py:275
  180.4 0.6 shard_map.117
  181.0 17.4 %collective-permute-start.15 = (bf16[1,64,3584]{2,1,0:T(8,128)(2,1)S(1)}, bf16[1,64,3584]{2,1,0:T(8,128)(2,1)S(1)}, u32[]{:S(2)}, u32[]{:S(2)}) collective-permute-start(bf16[1,64,3584]{2,1,0:T(8,128)(2,1)S(1)} %bitcast.36), channel_id=1, source_target_pairs={{0,32},{32,64},{64,96},{96,128},{128,160},{160,192},{192,224},{224... | collective-permute-start | bytes 1376264 | tf_op jit(solution)/shard_map/ppermute | solution.py:33
  198.5 0.6 shard_map.118
  199.1 1.9 collective-permute-start.16
  201.0 6.3 %collective-permute-done.15 = bf16[1,64,3584]{2,1,0:T(8,128)(2,1)S(1)} collective-permute-done((bf16[1,64,3584]{2,1,0:T(8,128)(2,1)S(1)}, bf16[1,64,3584]{2,1,0:T(8,128)(2,1)S(1)}, u32[]{:S(2)}, u32[]{:S(2)}) %collective-permute-start.15) | collective-permute-done | bytes 458784 | tf_op jit(solution)/shard_map/ppermute | solution.py:33
  207.2 11.1 %collective-permute-done.16 = bf16[1,64,3584]{2,1,0:T(8,128)(2,1)S(1)} collective-permute-done((bf16[1,64,3584]{2,1,0:T(8,128)(2,1)S(1)}, bf16[1,64,3584]{2,1,0:T(8,128)(2,1)S(1)}, u32[]{:S(2)}, u32[]{:S(2)}) %collective-permute-start.16) | collective-permute-done | bytes 458784 | tf_op jit(solution)/shard_map/ppermute | solution.py:33
  218.3 0.8 copy.16
  219.1 0.8 copy.17
  (37 shorter events, 0.2 us)
Async XLA Ops:
  0.6 0.7 copy-start.13
  0.6 0.7 copy-start.14
  1.3 1.0 copy-start.2
  2.3 1.0 copy-start.4
  3.3 0.7 copy-start.12
  5.9 7.0 %copy-start = (bf16[1,3584,128]{2,1,0:T(8,128)(2,1)S(1)}, bf16[1,3584,128]{2,1,0:T(8,128)(2,1)}, u32[]{:S(2)}) copy-start(bf16[1,3584,128]{2,1,0:T(8,128)(2,1)} %param.17) | copy-start | bytes 2752516
  5.9 39.1 %all-to-all-start = ((bf16[8,120,512]{2,1,0:T(8,128)(2,1)}), bf16[8,120,512]{2,1,0:T(8,128)(2,1)S(1)}, u32[]{:S(2)}, u32[]{:S(2)}) async-start(bf16[8,120,512]{2,1,0:T(8,128)(2,1)} %shard_map.113), calls=%async_computation | async-start | bytes 1966080 | tf_op jit(solution)/shard_map/all_to_all | solution.py:238
  12.9 4.9 %copy-start.15 = (bf16[1,128,3584]{2,1,0:T(8,128)(2,1)S(1)}, bf16[1,128,3584]{2,1,0:T(8,128)(2,1)}, u32[]{:S(2)}) copy-start(bf16[1,128,3584]{2,1,0:T(8,128)(2,1)} %param.19) | copy-start | bytes 2752516
  13.7 31.3 %collective-permute-start = (bf16[2048,128]{1,0:T(8,128)(2,1)}, bf16[2048,128]{1,0:T(8,128)(2,1)S(1)}, u32[]{:S(2)}, u32[]{:S(2)}) collective-permute-start(bf16[2048,128]{1,0:T(8,128)(2,1)} %slice_bitcast_fusion), channel_id=1, source_target_pairs={{0,1},{1,0},{2,3},{3,2},{4,5},{5,4},{6,7},{7,6},{8,9},{9,8},{10,11... | collective-permute-start | bytes 1572872 | tf_op jit(solution)/shard_map/ppermute | solution.py:38
  18.7 30.3 %copy-start.1 = (bf16[1,3584,128]{2,1,0:T(8,128)(2,1)S(1)}, bf16[1,3584,128]{2,1,0:T(8,128)(2,1)}, u32[]{:S(2)}) copy-start(bf16[1,3584,128]{2,1,0:T(8,128)(2,1)} %param.18) | copy-start | bytes 2752516
  18.8 25.5 %collective-permute-start.1 = (bf16[2,128,896]{2,1,0:T(8,128)(2,1)S(1)}, bf16[2,128,896]{2,1,0:T(8,128)(2,1)S(1)}, u32[]{:S(2)}, u32[]{:S(2)}) collective-permute-start(bf16[2,128,896]{2,1,0:T(8,128)(2,1)S(1)} %pad_maximum_fusion.1), channel_id=1, source_target_pairs={{0,2},{1,3},{2,0},{3,1},{4,6},{5,7},{6,4},{7,5},{8,10},{9,11},{10,... | collective-permute-start | bytes 1376264 | tf_op jit(solution)/shard_map/ppermute | solution.py:38
  44.2 0.8 copy-start.18
  45.0 10.5 %copy-start.17 = (bf16[1,128,896]{2,1,0:T(8,128)(2,1)S(1)}, bf16[1,128,896]{2,1,0:T(8,128)(2,1)}, u32[]{:S(2)}) copy-start(bf16[1,128,896]{2,1,0:T(8,128)(2,1)} %get-tuple-element.34) | copy-start | bytes 688132
  45.0 55.9 %collective-permute-start.2 = (bf16[8,120,512]{2,1,0:T(8,128)(2,1)S(1)}, bf16[8,120,512]{2,1,0:T(8,128)(2,1)S(1)}, u32[]{:S(2)}, u32[]{:S(2)}) collective-permute-start(bf16[8,120,512]{2,1,0:T(8,128)(2,1)S(1)} %all-to-all-done.refs_0_), channel_id=1, source_target_pairs={{0,4},{1,5},{2,6},{3,7},{4,0},{5,1},{6,2},{7,3},{8,12},{9,13},{10,... | collective-permute-start | bytes 2949128 | tf_op jit(solution)/shard_map/ppermute | solution.py:38
  47.1 58.6 %collective-permute-start.6 = (bf16[8,120,512]{2,1,0:T(8,128)(2,1)S(1)}, bf16[8,120,512]{2,1,0:T(8,128)(2,1)S(1)}, u32[]{:S(2)}, u32[]{:S(2)}) collective-permute-start(bf16[8,120,512]{2,1,0:T(8,128)(2,1)S(1)} %all-to-all-done.refs_0_), channel_id=1, source_target_pairs={{0,2},{1,3},{2,0},{3,1},{4,6},{5,7},{6,4},{7,5},{8,10},{9,11},{10,... | collective-permute-start | bytes 2949128 | tf_op jit(solution)/shard_map/ppermute | solution.py:38
  49.0 51.9 %collective-permute-start.4 = (bf16[3584,128]{1,0:T(8,128)(2,1)S(1)}, bf16[3584,128]{1,0:T(8,128)(2,1)S(1)}, u32[]{:S(2)}, u32[]{:S(2)}) collective-permute-start(bf16[3584,128]{1,0:T(8,128)(2,1)S(1)} %bitcast.29), channel_id=1, source_target_pairs={{0,1},{1,0},{2,3},{3,2},{4,5},{5,4},{6,7},{7,6},{8,9},{9,8},{10,11... | collective-permute-start | bytes 2752520 | tf_op jit(solution)/shard_map/ppermute | solution.py:38
  55.5 2.4 %copy-start.19 = (bf16[1536,128]{1,0:T(8,128)(2,1)S(1)}, bf16[1536,128]{1,0:T(8,128)(2,1)}, u32[]{:S(2)}) copy-start(bf16[1536,128]{1,0:T(8,128)(2,1)} %slice_bitcast_fusion.1) | copy-start | bytes 1179652
  55.6 45.3 %collective-permute-start.3 = (bf16[2,128,896]{2,1,0:T(8,128)(2,1)S(1)}, bf16[2,128,896]{2,1,0:T(8,128)(2,1)S(1)}, u32[]{:S(2)}, u32[]{:S(2)}) collective-permute-start(bf16[2,128,896]{2,1,0:T(8,128)(2,1)S(1)} %pad_maximum_fusion.2), channel_id=1, source_target_pairs={{0,4},{1,5},{2,6},{3,7},{4,0},{5,1},{6,2},{7,3},{8,12},{9,13},{10,... | collective-permute-start | bytes 1376264 | tf_op jit(solution)/shard_map/ppermute | solution.py:38
  58.0 42.9 %collective-permute-start.5 = (bf16[1536,128]{1,0:T(8,128)(2,1)S(1)}, bf16[1536,128]{1,0:T(8,128)(2,1)S(1)}, u32[]{:S(2)}, u32[]{:S(2)}) collective-permute-start(bf16[1536,128]{1,0:T(8,128)(2,1)S(1)} %copy-done.19), channel_id=1, source_target_pairs={{0,1},{1,0},{2,3},{3,2},{4,5},{5,4},{6,7},{7,6},{8,9},{9,8},{10,11... | collective-permute-start | bytes 1179656 | tf_op jit(solution)/shard_map/ppermute | solution.py:38
  102.1 5.5 %copy-start.16 = (bf16[1,128,896]{2,1,0:T(8,128)(2,1)S(1)}, bf16[1,128,896]{2,1,0:T(8,128)(2,1)}, u32[]{:S(2)}) copy-start(bf16[1,128,896]{2,1,0:T(8,128)(2,1)} %get-tuple-element.32) | copy-start | bytes 688132
  102.1 6.0 %collective-permute-start.8 = (bf16[272,256]{1,0:T(8,128)(2,1)S(1)}, bf16[272,256]{1,0:T(8,128)(2,1)S(1)}, u32[]{:S(2)}, u32[]{:S(2)}) collective-permute-start(bf16[272,256]{1,0:T(8,128)(2,1)S(1)} %shard_map.114.refs_0_), channel_id=1, source_target_pairs={{0,4},{1,5},{2,6},{3,7},{4,0},{5,1},{6,2},{7,3},{8,12},{9,13},{10,... | collective-permute-start | bytes 417800 | tf_op jit(solution)/shard_map/ppermute | solution.py:38
  105.7 26.1 %collective-permute-start.7 = (bf16[8,120,512]{2,1,0:T(8,128)(2,1)S(1)}, bf16[8,120,512]{2,1,0:T(8,128)(2,1)S(1)}, u32[]{:S(2)}, u32[]{:S(2)}) collective-permute-start(bf16[8,120,512]{2,1,0:T(8,128)(2,1)S(1)} %collective-permute-done.6.refs_0_), channel_id=1, source_target_pairs={{0,4},{1,5},{2,6},{3,7},{4,0},{5,1},{6,2},{7,3},{8,12},{9,13},{10,... | collective-permute-start | bytes 2949128 | tf_op jit(solution)/shard_map/ppermute | solution.py:38
  108.1 25.5 %copy-start.6 = (bf16[272,256]{1,0:T(8,128)(2,1)}, bf16[272,256]{1,0:T(8,128)(2,1)S(1)}, u32[]{:S(2)}) copy-start(bf16[272,256]{1,0:T(8,128)(2,1)S(1)} %collective-permute-done.8.refs_2_) | copy-start | bytes 417796
  108.1 36.6 %collective-permute-start.14 = (bf16[4,128,896]{2,1,0:T(8,128)(2,1)S(1)}, bf16[4,128,896]{2,1,0:T(8,128)(2,1)}, u32[]{:S(2)}, u32[]{:S(2)}) collective-permute-start(bf16[4,128,896]{2,1,0:T(8,128)(2,1)S(1)} %pad_maximum_fusion.refs_8_), channel_id=1, source_target_pairs={{0,1},{1,0},{2,3},{3,2},{4,5},{5,4},{6,7},{7,6},{8,9},{9,8},{10,11... | collective-permute-start | bytes 2752520 | tf_op jit(solution)/shard_map/ppermute | solution.py:38
  110.0 17.1 %collective-permute-start.9 = (bf16[272,256]{1,0:T(8,128)(2,1)S(1)}, bf16[272,256]{1,0:T(8,128)(2,1)S(1)}, u32[]{:S(2)}, u32[]{:S(2)}) collective-permute-start(bf16[272,256]{1,0:T(8,128)(2,1)S(1)} %shard_map.114.refs_0_), channel_id=1, source_target_pairs={{0,2},{1,3},{2,0},{3,1},{4,6},{5,7},{6,4},{7,5},{8,10},{9,11},{10,... | collective-permute-start | bytes 417800 | tf_op jit(solution)/shard_map/ppermute | solution.py:38
  114.2 17.5 %collective-permute-start.10 = (bf16[272,256]{1,0:T(8,128)(2,1)S(1)}, bf16[272,256]{1,0:T(8,128)(2,1)S(1)}, u32[]{:S(2)}, u32[]{:S(2)}) collective-permute-start(bf16[272,256]{1,0:T(8,128)(2,1)S(1)} %shard_map.114.refs_0_), channel_id=1, source_target_pairs={{0,6},{1,7},{2,4},{3,5},{4,2},{5,3},{6,0},{7,1},{8,14},{9,15},{10,... | collective-permute-start | bytes 417800 | tf_op jit(solution)/shard_map/ppermute | solution.py:38
  127.1 6.5 %copy-start.8 = (bf16[272,256]{1,0:T(8,128)(2,1)}, bf16[272,256]{1,0:T(8,128)(2,1)S(1)}, u32[]{:S(2)}) copy-start(bf16[272,256]{1,0:T(8,128)(2,1)S(1)} %collective-permute-done.9.refs_4_) | copy-start | bytes 417796
  131.7 1.9 copy-start.10
  133.6 11.1 %collective-permute-start.11 = (bf16[272,256]{1,0:T(8,128)(2,1)}, bf16[272,256]{1,0:T(8,128)(2,1)S(1)}, u32[]{:S(2)}, u32[]{:S(2)}) collective-permute-start(bf16[272,256]{1,0:T(8,128)(2,1)} %shard_map.115.refs_1_), channel_id=1, source_target_pairs={{0,4},{1,5},{2,6},{3,7},{4,0},{5,1},{6,2},{7,3},{8,12},{9,13},{10,... | collective-permute-start | bytes 417800 | tf_op jit(solution)/shard_map/ppermute | solution.py:38
  136.5 8.2 %collective-permute-start.12 = (bf16[272,256]{1,0:T(8,128)(2,1)}, bf16[272,256]{1,0:T(8,128)(2,1)S(1)}, u32[]{:S(2)}, u32[]{:S(2)}) collective-permute-start(bf16[272,256]{1,0:T(8,128)(2,1)} %shard_map.115.refs_1_), channel_id=1, source_target_pairs={{0,2},{1,3},{2,0},{3,1},{4,6},{5,7},{6,4},{7,5},{8,10},{9,11},{10,... | collective-permute-start | bytes 417800 | tf_op jit(solution)/shard_map/ppermute | solution.py:38
  141.5 8.8 %collective-permute-start.13 = (bf16[272,256]{1,0:T(8,128)(2,1)}, bf16[272,256]{1,0:T(8,128)(2,1)S(1)}, u32[]{:S(2)}, u32[]{:S(2)}) collective-permute-start(bf16[272,256]{1,0:T(8,128)(2,1)} %shard_map.115.refs_1_), channel_id=1, source_target_pairs={{0,6},{1,7},{2,4},{3,5},{4,2},{5,3},{6,0},{7,1},{8,14},{9,15},{10,... | collective-permute-start | bytes 417800 | tf_op jit(solution)/shard_map/ppermute | solution.py:38
  150.3 0.9 copy-start.7
  151.2 0.9 copy-start.9
  152.1 0.9 copy-start.11
  156.7 23.7 %copy-start.3 = (bf16[1,64,3584]{2,1,0:T(8,128)(2,1)S(1)}, bf16[1,64,3584]{2,1,0:T(8,128)(2,1)}, u32[]{:S(2)}) copy-start(bf16[1,64,3584]{2,1,0:T(8,128)(2,1)} %param.10) | copy-start | bytes 1376260
  156.7 23.7 %all-to-all-start.1 = ((bf16[16,2,120,128]{3,2,1,0:T(8,128)(2,1)}), bf16[16,2,120,128]{3,2,1,0:T(8,128)(2,1)S(1)}, u32[]{:S(2)}, u32[]{:S(2)}) async-start(bf16[16,2,120,128]{3,2,1,0:T(8,128)(2,1)} %shard_map.116), calls=%async_computation.1 | async-start | bytes 1966080 | tf_op jit(solution)/shard_map/all_to_all | solution.py:275
  160.7 0.7 copy-start.20
  161.4 0.7 copy-start.21
  162.2 36.3 %copy-start.5 = (bf16[1,64,3584]{2,1,0:T(8,128)(2,1)S(1)}, bf16[1,64,3584]{2,1,0:T(8,128)(2,1)}, u32[]{:S(2)}) copy-start(bf16[1,64,3584]{2,1,0:T(8,128)(2,1)} %param.11) | copy-start | bytes 1376260
  181.0 26.2 %collective-permute-start.15 = (bf16[1,64,3584]{2,1,0:T(8,128)(2,1)S(1)}, bf16[1,64,3584]{2,1,0:T(8,128)(2,1)S(1)}, u32[]{:S(2)}, u32[]{:S(2)}) collective-permute-start(bf16[1,64,3584]{2,1,0:T(8,128)(2,1)S(1)} %bitcast.36), channel_id=1, source_target_pairs={{0,32},{32,64},{64,96},{96,128},{128,160},{160,192},{192,224},{224... | collective-permute-start | bytes 1376264 | tf_op jit(solution)/shard_map/ppermute | solution.py:33
  199.1 19.2 %collective-permute-start.16 = (bf16[1,64,3584]{2,1,0:T(8,128)(2,1)S(1)}, bf16[1,64,3584]{2,1,0:T(8,128)(2,1)S(1)}, u32[]{:S(2)}, u32[]{:S(2)}) collective-permute-start(bf16[1,64,3584]{2,1,0:T(8,128)(2,1)S(1)} %bitcast.37), channel_id=1, source_target_pairs={{0,480},{32,0},{64,32},{96,64},{128,96},{160,128},{192,160},{224,1... | collective-permute-start | bytes 1376264 | tf_op jit(solution)/shard_map/ppermute | solution.py:33
